TPU v7x, 512 devices: a whole 4x4x16 slice. The times are simulated.
512 devices in a mesh: grp: 8 (over x, core), slab: 64 (over y, z).
Axes of the slice: x: 4, y: 4, z: 16, core: 2. Of those that a mesh axis runs over, the one named last changes fastest.
Arguments:
- nodes: bfloat16 [8, 16384, 128], P('grp', 'slab'), may hold values from -6 to 6
- leave_list: int32 [8, 4096], P('grp', 'slab'), may hold values from 0 to 255, as said below
- arrive_list: int32 [8, 16384], P('grp', 'slab'), may hold values from 0 to 319, as said below
- send_list: int32 [8, 8192], P('grp', 'slab'), may hold values from 0 to 255
- neighbours: int32 [8, 16384, 32], P('grp', 'slab'), may hold values from 0 to 383
- valid: int32 [8, 16384, 32], P('grp', 'slab'), may hold values 0 or 1
- w_send: bfloat16 [128, 128], replicated, may hold values from -0.5 to 0.5
- w_recv: bfloat16 [128, 128], replicated, may hold values from -0.5 to 0.5
- w_msg: bfloat16 [128, 128], replicated, may hold values from -0.5 to 0.5
- w_self: bfloat16 [128, 128], replicated, may hold values from -0.5 to 0.5
- w_agg: bfloat16 [128, 128], replicated, may hold values from -0.09375 to 0.09375
- w_out: bfloat16 [128, 128], replicated, may hold values from -0.5 to 0.5
- cotangent: bfloat16 [8, 16384, 128], P('grp', 'slab'), may hold values from -6 to 6
Outputs:
- updated: bfloat16 [8, 16384, 128], P('grp', 'slab')
- grad_nodes: bfloat16 [8, 16384, 128], P('grp', 'slab')
- weight_steps: float32 [6, 128, 128], replicated
Inputs may be any that keep to these rules, and one draw needn't show every extreme that they name: `leave_list`: each slab's 2 * 32 entries are distinct rows of that slab. `arrive_list`: each slab's 256 entries are distinct; they name every incoming row (entries 256 and above) and every own row not in that slab's leave_list, and nothing else.
All inputs are finite; a program needn't handle non-finite values. No bound on the sum of `valid` on one device may be relied on, other than what follows from the above.
Results may differ from a plain program's by a relative error of at most 0.0065.
Values may be sent and summed in bfloat16 or wider, within the bound.
A program may use at most 64 MiB of HBM per device.

v0:
```python
import math

import jax
import jax.numpy as jnp
from jax import lax
from jax.sharding import PartitionSpec as P


def with_halo(array, sides, width):
    for axis, dim in sides:
        size, length = (lax.axis_size(axis), array.shape[dim])
        up = [(i, (i + 1) % size) for i in range(size)]
        down = [(j, i) for i, j in up]
        last = lax.slice_in_dim(array, length - width, length, axis=dim)
        first = lax.slice_in_dim(array, 0, width, axis=dim)
        before = lax.ppermute(last, axis, up)
        after = lax.ppermute(first, axis, down)
        array = jnp.concatenate([before, array, after], axis=dim)
    return array


def dsilu(value):
    sig = jax.nn.sigmoid(value)
    return sig * (1.0 + value * (1.0 - sig))


def inner(left, right):
    return lax.dot_general(
        left, right, (((0,), (0,)), ((), ())), preferred_element_type=jnp.float32
    )


def by_transpose(left, right):
    return lax.dot_general(
        left, right, (((1,), (1,)), ((), ())), preferred_element_type=jnp.float32
    )


def normalize(total):
    return total / jnp.sqrt(jnp.mean(total * total, axis=(1, 2), keepdims=True) + 1e-06)


def shards(
    nodes,
    leave_list,
    arrive_list,
    send_list,
    neighbours,
    valid,
    w_send,
    w_recv,
    w_msg,
    w_self,
    w_agg,
    w_out,
    cotangent,
):
    plain = nodes[0]
    leave = leave_list[0]
    migr = leave.shape[0] // 2
    moving = jnp.take(plain, leave, axis=0)
    arrived = with_halo(moving, (("slab", 0),), migr)
    pool = jnp.concatenate([plain, arrived[:migr], arrived[3 * migr :]], axis=0)
    moved = jnp.take(pool, arrive_list[0], axis=0)
    sends = send_list[0]
    border = sends.shape[0] // 2
    outgoing = jnp.take(moved, sends, axis=0)
    beside_all = with_halo(outgoing, (("slab", 0),), border)
    table = jnp.concatenate([moved, beside_all[:border], beside_all[3 * border :]], axis=0)
    table_rows = table.shape[0]
    rows, width = moved.shape
    nbr = neighbours[0]
    slots = nbr.shape[1]
    maskf = valid[0].astype(jnp.float32)
    cot = cotangent[0]
    block = math.gcd(rows, 64)
    blocks = rows // block
    centre = jnp.dot(moved, w_send, preferred_element_type=jnp.float32)
    neigh = jnp.dot(table, w_recv, preferred_element_type=jnp.float32).astype(jnp.bfloat16)
    centre_blocks = centre.reshape(blocks, block, width)
    nbr_blocks = nbr.reshape(blocks, block, slots)
    mask_blocks = maskf.reshape(blocks, block, slots)

    def edge_front(centre_blk, nbr_blk):
        gathered = jnp.take(neigh, nbr_blk.reshape(-1), axis=0).reshape(block, slots, width)
        pre = centre_blk[:, None, :] + gathered.astype(jnp.float32)
        hid = jax.nn.silu(pre).astype(jnp.bfloat16).reshape(-1, width)
        pre2 = jnp.dot(hid, w_msg, preferred_element_type=jnp.float32).reshape(block, slots, width)
        return (pre, hid, pre2)

    def aggregate(item):
        pre, hid, pre2 = edge_front(item[0], item[1])
        return jnp.sum(item[2][:, :, None] * jax.nn.silu(pre2), axis=1)

    agg = lax.map(aggregate, (centre_blocks, nbr_blocks, mask_blocks)).reshape(rows, width)
    agg_b = agg.astype(jnp.bfloat16)
    node_pre = jnp.dot(moved, w_self, preferred_element_type=jnp.float32) + jnp.dot(
        agg_b, w_agg, preferred_element_type=jnp.float32
    )
    node_hid = jax.nn.silu(node_pre).astype(jnp.bfloat16)
    updated = (
        moved.astype(jnp.float32) + jnp.dot(node_hid, w_out, preferred_element_type=jnp.float32)
    ).astype(jnp.bfloat16)
    g_out = inner(node_hid, cot)
    d_node_pre = (by_transpose(cot, w_out) * dsilu(node_pre)).astype(jnp.bfloat16)
    g_self = inner(moved, d_node_pre)
    g_agg = inner(agg_b, d_node_pre)
    d_agg_blocks = by_transpose(d_node_pre, w_agg).reshape(blocks, block, width)

    def edge_back(carry, item):
        g_msg_part, d_neigh_part = carry
        centre_blk, nbr_blk, mask_blk, d_agg_blk = item
        pre, hid, pre2 = edge_front(centre_blk, nbr_blk)
        d_pre2 = (
            (mask_blk[:, :, None] * d_agg_blk[:, None, :] * dsilu(pre2))
            .astype(jnp.bfloat16)
            .reshape(-1, width)
        )
        g_msg_part = g_msg_part + inner(hid, d_pre2)
        d_pre = by_transpose(d_pre2, w_msg).reshape(block, slots, width) * dsilu(pre)
        d_neigh_part = d_neigh_part + jax.ops.segment_sum(
            d_pre.reshape(-1, width), nbr_blk.reshape(-1), num_segments=table_rows
        )
        return ((g_msg_part, d_neigh_part), jnp.sum(d_pre, axis=1))

    start = (jnp.zeros((width, width), jnp.float32), jnp.zeros((table_rows, width), jnp.float32))
    (g_msg, d_neigh_sum), d_centre_blocks = lax.scan(
        edge_back, start, (centre_blocks, nbr_blocks, mask_blocks, d_agg_blocks)
    )
    d_centre = d_centre_blocks.reshape(rows, width).astype(jnp.bfloat16)
    d_neigh = d_neigh_sum.astype(jnp.bfloat16)
    g_recv = inner(table, d_neigh)
    g_send = inner(moved, d_centre)
    d_own = by_transpose(d_neigh[:rows], w_recv)
    d_local = (
        cot.astype(jnp.float32)
        + by_transpose(d_node_pre, w_self)
        + by_transpose(d_centre, w_send)
        + d_own
    )
    d_borrowed = by_transpose(d_neigh[rows:], w_recv)
    returned = with_halo(d_borrowed.astype(jnp.bfloat16), (("slab", 0),), border).astype(
        d_borrowed.dtype
    )
    from_lower = returned[:border]
    from_upper = returned[3 * border :]
    d_local = d_local.at[sends[:border]].add(from_lower)
    d_local = d_local.at[sends[border:]].add(from_upper)
    grad_nodes = d_local.astype(jnp.bfloat16)
    grads = jnp.stack([g_send, g_recv, g_msg, g_self, g_agg, g_out])
    total = lax.psum(grads, ("grp", "slab"))
    weight_steps = normalize(total)
    return (updated[None], grad_nodes[None], weight_steps)


def solution(mesh):
    in_specs = (
        P("grp", "slab", None),
        P("grp", "slab"),
        P("grp", "slab"),
        P("grp", "slab"),
        P("grp", "slab", None),
        P("grp", "slab", None),
        P(),
        P(),
        P(),
        P(),
        P(),
        P(),
        P("grp", "slab", None),
    )
    out_specs = (P("grp", "slab", None), P("grp", "slab", None), P())
    return jax.shard_map(shards, mesh=mesh, in_specs=in_specs, out_specs=out_specs, check_vma=False)
```

profile of v0, /device:TPU:1, one launch (start us, length us, event | category | flops | bytes accessed | tf_op | source)
XLA Modules:
  0.0 654.5 jit_solution(8680873252876542450)
XLA Ops:
  10.1 4.4 collective-permute-start
  14.5 11.9 %collective-permute-start.1 = (bf16[32,128]{1,0:T(8,128)(2,1)S(1)}, bf16[32,128]{1,0:T(8,128)(2,1)S(1)}, u32[]{:S(2)}, u32[]{:S(2)}) collective-permute-start(bf16[32,128]{1,0:T(8,128)(2,1)S(1)} %get-tuple-element.175), channel_id=1, source_target_pairs={{1,0},{2,1},{3,2},{4,3},{5,4},{6,5},{7,6},{8,7},{9,8},{10,9},{11,1... | collective-permute-start | bytes 24584 | tf_op jit(solution)/shard_map/ppermute | solution.py:17
  30.6 1.9 collective-permute-start.2
  32.6 6.7 %collective-permute-start.3 = (bf16[64,128]{1,0:T(8,128)(2,1)S(1)}, bf16[64,128]{1,0:T(8,128)(2,1)S(1)}, u32[]{:S(2)}, u32[]{:S(2)}) collective-permute-start(bf16[64,128]{1,0:T(8,128)(2,1)S(1)} %get-tuple-element.173), channel_id=1, source_target_pairs={{1,0},{2,1},{3,2},{4,3},{5,4},{6,5},{7,6},{8,7},{9,8},{10,9},{11,1... | collective-permute-start | bytes 49160 | tf_op jit(solution)/shard_map/ppermute | solution.py:17
  40.7 32.7 %while.25 = (s32[]{:T(128)}, bf16[4,64,128]{2,1,0:T(8,128)(2,1)S(1)}, f32[4,64,32]{2,1,0:T(8,128)S(1)}, f32[4,64,128]{2,1,0:T(8,128)S(1)}, s32[4,64,32]{2,1,0:T(...) while((s32[]{:T(128)}, bf16[4,64,128]{2,1,0:T(8,128)(2,1)S(1)}, ...), condition=%wide.region_2.4_spmd, body=%wide.region_0.3_spmd.sunk | while | flops 70791168 | bytes 2895973 | solution.py:95
  40.8 6.2 gather_fusion
  49.0 6.2 gather_fusion
  57.2 6.2 gather_fusion
  65.4 6.2 gather_fusion
  78.4 101.8 %while.26 = (s32[]{:T(128)}, f32[128,128]{1,0:T(8,128)}, f32[384,128]{1,0:T(8,128)S(1)}, bf16[4,64,128]{2,1,0:T(8,128)(2,1)}, f32[4,64,128]{2,1,0:T(8,128)S(1)},...) while((s32[]{:T(128)}, f32[128,128]{1,0:T(8,128)}, ...), condition=%wide.region_6.8_spmd.clone, body=%wide.region_3.7_spmd.clone.sunk | while | flops 211070976 | bytes 15293151 | solution.py:127
  78.4 6.2 gather_fusion.1
  89.5 11.6 %scatter_fusion = f32[384,128]{1,0:T(8,128)S(1)} fusion(f32[384,128]{1,0:T(8,128)S(1)} %get-tuple-element.330, s32[2048]{0:T(1024)S(1)} %reshape.334, f32[2048,128]{1,0:T(8,128)S(1)} %bitcast.171), kind=kCustom, calls=%fused_computation.5.clone.clone.1 | custom fusion | flops 262144 | bytes 3153920 | tf_op jit(solution)/shard_map/while/body/eval_jaxpr/scatter-add | solution.py:121
  103.9 6.2 gather_fusion.1
  114.9 11.6 %scatter_fusion = f32[384,128]{1,0:T(8,128)S(1)} fusion(f32[384,128]{1,0:T(8,128)S(1)} %get-tuple-element.330, s32[2048]{0:T(1024)S(1)} %reshape.334, f32[2048,128]{1,0:T(8,128)S(1)} %bitcast.171), kind=kCustom, calls=%fused_computation.5.clone.clone.1 | custom fusion | flops 262144 | bytes 3153920 | tf_op jit(solution)/shard_map/while/body/eval_jaxpr/scatter-add | solution.py:121
  127.1 1.5 fusion.88
  129.4 6.2 gather_fusion.1
  140.4 11.6 %scatter_fusion = f32[384,128]{1,0:T(8,128)S(1)} fusion(f32[384,128]{1,0:T(8,128)S(1)} %get-tuple-element.330, s32[2048]{0:T(1024)S(1)} %reshape.334, f32[2048,128]{1,0:T(8,128)S(1)} %bitcast.171), kind=kCustom, calls=%fused_computation.5.clone.clone.1 | custom fusion | flops 262144 | bytes 3153920 | tf_op jit(solution)/shard_map/while/body/eval_jaxpr/scatter-add | solution.py:121
  152.6 1.5 fusion.88
  154.8 6.2 gather_fusion.1
  165.8 11.6 %scatter_fusion = f32[384,128]{1,0:T(8,128)S(1)} fusion(f32[384,128]{1,0:T(8,128)S(1)} %get-tuple-element.330, s32[2048]{0:T(1024)S(1)} %reshape.334, f32[2048,128]{1,0:T(8,128)S(1)} %bitcast.171), kind=kCustom, calls=%fused_computation.5.clone.clone.1 | custom fusion | flops 262144 | bytes 3153920 | tf_op jit(solution)/shard_map/while/body/eval_jaxpr/scatter-add | solution.py:121
  178.0 1.5 fusion.88
  186.1 1.9 collective-permute-start.4
  188.0 7.0 %collective-permute-start.5 = (bf16[64,128]{1,0:T(8,128)(2,1)S(1)}, bf16[64,128]{1,0:T(8,128)(2,1)S(1)}, u32[]{:S(2)}, u32[]{:S(2)}) collective-permute-start(bf16[64,128]{1,0:T(8,128)(2,1)S(1)} %get-tuple-element.171), channel_id=1, source_target_pairs={{1,0},{2,1},{3,2},{4,3},{5,4},{6,5},{7,6},{8,7},{9,8},{10,9},{11,1... | collective-permute-start | bytes 49160 | tf_op jit(solution)/shard_map/ppermute | solution.py:17
  198.4 447.1 %all-reduce.2.cloned.1.call-done = f32[6,128,128]{2,1,0:T(8,128)} async-done(((f32[6,128,128]{2,1,0:T(8,128)}), f32[6,128,128]{2,1,0:T(8,128)}) %all-reduce.2.cloned.1.call-update) | async-done | bytes 393232 | tf_op jit(solution)/shard_map/psum | solution.py:151
  (215 shorter events, 58.2 us)
Async XLA Ops:
  7.2 32.9 %copy-start = (bf16[128,128]{1,0:T(8,128)(2,1)S(1)}, bf16[128,128]{1,0:T(8,128)(2,1)}, u32[]{:S(2)}) copy-start(bf16[128,128]{1,0:T(8,128)(2,1)} %param.26) | copy-start | bytes 98308
  7.2 638.4 %all-reduce.2.cloned.1.call-start = ((), (), s32[]{:S(2)}) async-start(), calls=%async_computation | async-start | bytes 786432 | tf_op jit(solution)/shard_map/psum | solution.py:151
  10.1 17.1 %copy-start.19 = (s32[1,256,32]{1,2,0:T(8,128)S(1)}, s32[1,256,32]{1,2,0:T(8,128)}, u32[]{:S(2)}) copy-start(s32[1,256,32]{1,2,0:T(8,128)} %param.24) | copy-start | bytes 98308
  10.1 18.0 %collective-permute-start = (bf16[32,128]{1,0:T(8,128)(2,1)S(1)}, bf16[32,128]{1,0:T(8,128)(2,1)S(1)}, u32[]{:S(2)}, u32[]{:S(2)}) collective-permute-start(bf16[32,128]{1,0:T(8,128)(2,1)S(1)} %get-tuple-element.174), channel_id=1, source_target_pairs={{0,1},{1,2},{2,3},{3,4},{4,5},{5,6},{6,7},{7,8},{8,9},{9,10},{10,1... | collective-permute-start | bytes 24584 | tf_op jit(solution)/shard_map/ppermute | solution.py:16
  14.5 13.6 %collective-permute-start.1 = (bf16[32,128]{1,0:T(8,128)(2,1)S(1)}, bf16[32,128]{1,0:T(8,128)(2,1)S(1)}, u32[]{:S(2)}, u32[]{:S(2)}) collective-permute-start(bf16[32,128]{1,0:T(8,128)(2,1)S(1)} %get-tuple-element.175), channel_id=1, source_target_pairs={{1,0},{2,1},{3,2},{4,3},{5,4},{6,5},{7,6},{8,7},{9,8},{10,9},{11,1... | collective-permute-start | bytes 24584 | tf_op jit(solution)/shard_map/ppermute | solution.py:17
  28.0 0.8 copy-start.4
  30.6 8.6 %copy-start.12 = (bf16[128,128]{1,0:T(8,128)(2,1)S(1)}, bf16[128,128]{1,0:T(8,128)(2,1)}, u32[]{:S(2)}) copy-start(bf16[128,128]{1,0:T(8,128)(2,1)} %param.25) | copy-start | bytes 98308
  30.6 8.8 %collective-permute-start.2 = (bf16[64,128]{1,0:T(8,128)(2,1)S(1)}, bf16[64,128]{1,0:T(8,128)(2,1)S(1)}, u32[]{:S(2)}, u32[]{:S(2)}) collective-permute-start(bf16[64,128]{1,0:T(8,128)(2,1)S(1)} %get-tuple-element.172), channel_id=1, source_target_pairs={{0,1},{1,2},{2,3},{3,4},{4,5},{5,6},{6,7},{7,8},{8,9},{9,10},{10,1... | collective-permute-start | bytes 49160 | tf_op jit(solution)/shard_map/ppermute | solution.py:16
  32.6 7.5 %collective-permute-start.3 = (bf16[64,128]{1,0:T(8,128)(2,1)S(1)}, bf16[64,128]{1,0:T(8,128)(2,1)S(1)}, u32[]{:S(2)}, u32[]{:S(2)}) collective-permute-start(bf16[64,128]{1,0:T(8,128)(2,1)S(1)} %get-tuple-element.173), channel_id=1, source_target_pairs={{1,0},{2,1},{3,2},{4,3},{5,4},{6,5},{7,6},{8,7},{9,8},{10,9},{11,1... | collective-permute-start | bytes 49160 | tf_op jit(solution)/shard_map/ppermute | solution.py:17
  39.4 0.9 copy-start.23
  40.7 32.7 %copy-start.8 = (bf16[128,128]{1,0:T(8,128)(2,1)S(1)}, bf16[128,128]{1,0:T(8,128)(2,1)}, u32[]{:S(2)}) copy-start(bf16[128,128]{1,0:T(8,128)(2,1)} %param.29) | copy-start | bytes 98308
  74.2 0.8 copy-start.22
  75.1 1.8 copy-start.9
  89.5 12.2 %copy-start.13 = (f32[128,128]{1,0:T(8,128)S(1)}, f32[128,128]{1,0:T(8,128)}, u32[]{:S(2)}) copy-start(f32[128,128]{1,0:T(8,128)} %get-tuple-element.329) | copy-start | bytes 196612 | tf_op jit(solution)/shard_map/while
  114.9 12.2 %copy-start.13 = (f32[128,128]{1,0:T(8,128)S(1)}, f32[128,128]{1,0:T(8,128)}, u32[]{:S(2)}) copy-start(f32[128,128]{1,0:T(8,128)} %get-tuple-element.329) | copy-start | bytes 196612 | tf_op jit(solution)/shard_map/while
  140.4 12.2 %copy-start.13 = (f32[128,128]{1,0:T(8,128)S(1)}, f32[128,128]{1,0:T(8,128)}, u32[]{:S(2)}) copy-start(f32[128,128]{1,0:T(8,128)} %get-tuple-element.329) | copy-start | bytes 196612 | tf_op jit(solution)/shard_map/while
  165.8 12.2 %copy-start.13 = (f32[128,128]{1,0:T(8,128)S(1)}, f32[128,128]{1,0:T(8,128)}, u32[]{:S(2)}) copy-start(f32[128,128]{1,0:T(8,128)} %get-tuple-element.329) | copy-start | bytes 196612 | tf_op jit(solution)/shard_map/while
  183.7 0.9 copy-start.10
  183.7 0.9 copy-start.17
  184.8 0.9 copy-start.5
  184.8 1.1 copy-start.7
  186.1 9.1 %collective-permute-start.4 = (bf16[64,128]{1,0:T(8,128)(2,1)S(1)}, bf16[64,128]{1,0:T(8,128)(2,1)S(1)}, u32[]{:S(2)}, u32[]{:S(2)}) collective-permute-start(bf16[64,128]{1,0:T(8,128)(2,1)S(1)} %get-tuple-element.170), channel_id=1, source_target_pairs={{0,1},{1,2},{2,3},{3,4},{4,5},{5,6},{6,7},{7,8},{8,9},{9,10},{10,1... | collective-permute-start | bytes 49160 | tf_op jit(solution)/shard_map/ppermute | solution.py:16
  188.0 7.8 %collective-permute-start.5 = (bf16[64,128]{1,0:T(8,128)(2,1)S(1)}, bf16[64,128]{1,0:T(8,128)(2,1)S(1)}, u32[]{:S(2)}, u32[]{:S(2)}) collective-permute-start(bf16[64,128]{1,0:T(8,128)(2,1)S(1)} %get-tuple-element.171), channel_id=1, source_target_pairs={{1,0},{2,1},{3,2},{4,3},{5,4},{6,5},{7,6},{8,7},{9,8},{10,9},{11,1... | collective-permute-start | bytes 49160 | tf_op jit(solution)/shard_map/ppermute | solution.py:17
  645.6 1.2 copy-start.1
  (21 other events, 15.3 us)
Sparse Core Ops, SparseCore 0:
  185.7 459.8 all-reduce.1
where the time goes:
time: 658 us; the launch traced here: 655 us
  waiting for transfers between devices  449 us (68%)
  local copies, waits for them, and re-layouts  71.9 us (11%)
  other arithmetic  57.9 us (9%)
  starting transfers between devices  33.8 us (5%)
  matrix products  27.3 us (4%)
  between operations  14.4 us (2%)
    psum x1, waiting for transfers between devices, shards(): total = lax.psum(grads, ('grp', 'slab'))  447 us
    gather x8, local copies, waits for them, and re-layouts, edge_front(): jnp.take(neigh, nbr_blk.reshape(-1), axis=0).reshape(block, slots, width)  49.4 us
    scatter-add x4, other arithmetic, edge_back(): jax.ops.segment_sum(d_pre.reshape(-1, width), nbr_blk.reshape(-1), num_se...  46.3 us
    ppermute x3, starting transfers between devices, with_halo(): after = lax.ppermute(first, axis, down)  25.6 us
  transfers between devices with their start and end apart: 7, of which 3 were waited for; matrix products, arithmetic and copies ran while one was open for 1% of the time, Pallas kernels for 0%

commit v1 on v0

v1 whole, which is shorter than its diff:
```python
import functools

import jax
import jax.numpy as jnp
from jax import lax
from jax.experimental import pallas as pl
from jax.experimental.pallas import tpu as pltpu
from jax.sharding import PartitionSpec as P

MESH = pl.DeviceIdType.MESH
F32 = jnp.float32
BF16 = jnp.bfloat16


def sigmoid(value):
    return 0.5 * jnp.tanh(0.5 * value) + 0.5


def dot(left, right):
    return lax.dot_general(left, right, (((1,), (0,)), ((), ())), preferred_element_type=F32)


def inner(left, right):
    return lax.dot_general(left, right, (((0,), (0,)), ((), ())), preferred_element_type=F32)


def by_transpose(left, right):
    return lax.dot_general(left, right, (((1,), (1,)), ((), ())), preferred_element_type=F32)


def hot(index, shape, dim):
    place = lax.broadcasted_iota(jnp.int32, shape, dim)
    return jnp.where(place == index, 1.0, 0.0).astype(BF16)


def bytes_of(ref, sem):
    return pltpu.make_async_copy(ref, ref, sem)


class Sum:
    def __init__(self, n_grp, n_y, n_z, mats, offset, scratch):
        self.n_grp, self.n_y, self.n_z = n_grp, n_y, n_z
        self.mats, self.offset = mats, offset
        self.plane = n_grp * n_y
        self.per, self.owners = shares(self.plane, mats)
        self.snd, self.rcv, self.part, self.zrcv, self.all, self.sems = scratch
        self.g = lax.axis_index("grp")
        slab = lax.axis_index("slab")
        self.y, self.z = slab // n_z, lax.rem(slab, n_z)
        self.q = self.g * n_y + self.y
        self.block = lax.rem(self.q + self.plane - offset, self.plane)
        self.is_owner = self.block < self.owners

    def device(self, q, z):
        return (q // self.n_y, lax.rem(q, self.n_y) * self.n_z + z)

    def copy(self, src, dst, phase, to):
        return pltpu.make_async_remote_copy(
            src_ref=src,
            dst_ref=dst,
            send_sem=self.sems.at[2 * phase],
            recv_sem=self.sems.at[2 * phase + 1],
            device_id=to,
            device_id_type=MESH,
        )

    def share(self, grads):
        tiles = 8
        for m in range(self.mats):
            low = grads[m].astype(BF16)
            for t in range(tiles):
                b = m * tiles + t
                self.snd[b // self.per, b % self.per] = low[t * 16 : (t + 1) * 16]

        def step(t, carry):
            block = lax.rem(self.block + t, self.plane)

            @pl.when(block < self.owners)
            def _():
                to = lax.rem(block + self.offset, self.plane)
                self.copy(
                    self.snd.at[block], self.rcv.at[self.plane - 1 - t], 0, self.device(to, self.z)
                ).start()

            return carry

        lax.fori_loop(1, self.plane, step, 0)

    def line(self):
        @pl.when(self.is_owner)
        def _():
            others = self.plane - 1
            bytes_of(self.rcv.at[pl.ds(0, others)], self.sems.at[1]).wait()
            total = self.snd[self.block].astype(F32)
            for i in range(others):
                total = total + self.rcv[i].astype(F32)
            self.part[0] = total.astype(BF16)
            self.zrcv[self.n_z - 1] = total.astype(BF16)
            half = self.n_z // 2

            def step(t, carry):
                to = lax.rem(self.z + half + t, self.n_z)
                slot = lax.rem(self.n_z - 1 - half - t + self.n_z, self.n_z)

                @pl.when(to != self.z)
                def _():
                    self.copy(
                        self.part.at[0], self.zrcv.at[slot], 1, self.device(self.q, to)
                    ).start()

                return carry

            lax.fori_loop(0, self.n_z, step, 0)

    def spread(self):
        @pl.when(self.is_owner)
        def _():
            bytes_of(self.zrcv.at[pl.ds(0, self.n_z - 1)], self.sems.at[3]).wait()
            total = jnp.zeros(self.part.shape[1:], F32)
            for i in range(self.n_z):
                total = total + self.zrcv[self.slot_of(i)].astype(F32)
            self.part[1] = total.astype(BF16)
            self.all[self.block] = total.astype(BF16)

            def step(t, carry):
                to = lax.rem(self.q + t, self.plane)
                self.copy(
                    self.part.at[1], self.all.at[self.block], 2, self.device(to, self.z)
                ).start()
                return carry

            lax.fori_loop(1, self.plane, step, 0)

    def slot_of(self, i):
        return lax.rem(self.n_z - 1 - (self.z - i) + 2 * self.n_z, self.n_z)

    def finish(self, out, first):
        own = self.is_owner

        @pl.when(own)
        def _():
            bytes_of(self.snd.at[pl.ds(0, self.owners - 1)], self.sems.at[0]).wait()
            bytes_of(self.zrcv.at[pl.ds(0, self.n_z - 1)], self.sems.at[2]).wait()
            bytes_of(self.rcv.at[pl.ds(0, self.plane - 1)], self.sems.at[4]).wait()
            if self.owners > 1:
                bytes_of(self.all.at[pl.ds(0, self.owners - 1)], self.sems.at[5]).wait()

        @pl.when(jnp.logical_not(own))
        def _():
            bytes_of(self.snd.at[pl.ds(0, self.owners)], self.sems.at[0]).wait()
            bytes_of(self.all.at[pl.ds(0, self.owners)], self.sems.at[5]).wait()

        for m in range(self.mats):
            tiles = []
            for t in range(8):
                b = m * 8 + t
                tiles.append(self.all[b // self.per, b % self.per])
            total = jnp.concatenate(tiles, axis=0).astype(F32)
            square = jnp.sum(jnp.sum(total * total, axis=0, keepdims=True), axis=1, keepdims=True)
            out[first + m] = total / jnp.sqrt(square * (1.0 / (128 * 128)) + 1e-06)


def shares(plane, mats):
    blocks = mats * 8
    per = -(-blocks // plane)
    while blocks % per:
        per += 1
    return per, blocks // per


def sum_scratch(plane, n_z, mats):
    per, owners = shares(plane, mats)
    return [
        pltpu.VMEM((owners, per, 16, 128), BF16),
        pltpu.VMEM((plane, per, 16, 128), BF16),
        pltpu.VMEM((2, per, 16, 128), BF16),
        pltpu.VMEM((n_z, per, 16, 128), BF16),
        pltpu.VMEM((owners, per, 16, 128), BF16),
        pltpu.SemaphoreType.DMA((6,)),
    ]


N_IN = 13
CH = 4


def kernel(n_grp, n_y, n_z, dims, *refs):
    rows, slots, migr, halo = dims
    table_rows = rows + 2 * halo
    ins = refs[:N_IN]
    updated_ref, grad_ref, steps_ref = refs[N_IN : N_IN + 3]
    scratch = refs[N_IN + 3 :]
    held = scratch[:N_IN]
    (
        in_sems,
        halo_sems,
        pool,
        mig_snd,
        out_snd,
        table,
        ret_snd,
        ret_rcv,
        col,
        row,
        oh,
        oht,
        mask,
        neigh,
        centre,
        agg,
        hid,
        ds1,
        md,
        d_agg,
        d_centre,
        d_neigh,
        g_msg,
    ) = scratch[N_IN : N_IN + 23]
    reduce_scratch = scratch[N_IN + 23 :]
    (nodes, leave, arrive, send, nbr, valid, w_send, w_recv, w_msg, w_self, w_agg, w_out, cot) = held

    g, slab = lax.axis_index("grp"), lax.axis_index("slab")
    n_slab = n_y * n_z
    y, z = slab // n_z, lax.rem(slab, n_z)
    plane = n_grp * n_y
    q = g * n_y + y
    lower = (g, lax.rem(slab + n_slab - 1, n_slab))
    upper = (g, lax.rem(slab + 1, n_slab))

    loads = [pltpu.make_async_copy(ins[i], held[i], in_sems.at[i]) for i in range(N_IN)]
    for i in range(N_IN):
        loads[i].start()

    barrier = pltpu.get_barrier_semaphore()
    for to in (lower, upper):
        pl.semaphore_signal(barrier, inc=1, device_id=to, device_id_type=MESH)

    def greet_plane(t, carry):
        to = lax.rem(q + t, plane)
        pl.semaphore_signal(
            barrier,
            inc=1,
            device_id=(to // n_y, lax.rem(to, n_y) * n_z + z),
            device_id_type=MESH,
        )
        return carry

    def greet_line(t, carry):
        to = (g, y * n_z + lax.rem(z + t, n_z))
        pl.semaphore_signal(barrier, inc=1, device_id=to, device_id_type=MESH)
        return carry

    lax.fori_loop(1, plane, greet_plane, 0)
    lax.fori_loop(1, n_z, greet_line, 0)

    def swap(src, low_src, low_dst, up_src, up_dst, dst, stage):
        size = low_src.size
        copies = []
        for k, (a, b, to) in enumerate(((low_src, low_dst, lower), (up_src, up_dst, upper))):
            copies.append(
                pltpu.make_async_remote_copy(
                    src_ref=src.at[a],
                    dst_ref=dst.at[b],
                    send_sem=halo_sems.at[4 * stage + k],
                    recv_sem=halo_sems.at[4 * stage + 2 + k],
                    device_id=to,
                    device_id_type=MESH,
                )
            )
        for copy in copies:
            copy.start()
        return copies

    loads[0].wait()
    loads[1].wait()
    mig_snd[...] = inner(hot(leave[...], (rows, 2 * migr), 0), nodes[...]).astype(BF16)
    pl.semaphore_wait(barrier, plane + n_z)
    moving = swap(
        mig_snd,
        pl.ds(0, migr),
        pl.ds(rows + migr, migr),
        pl.ds(migr, migr),
        pl.ds(rows, migr),
        pool,
        0,
    )
    pool[pl.ds(0, rows)] = nodes[...]
    for i in range(2, N_IN):
        loads[i].wait()
    arrive_hot = hot(arrive[...], (rows + 2 * migr, rows), 0)
    send_hot = hot(send[...], (rows, 2 * halo), 0)
    marked = jnp.where(valid[...] > 0, nbr[...], table_rows)
    col[:, pl.ds(0, slots)] = marked
    row[...] = col[...].T[0:slots]

    def front_hot(first, last):
        for k in range(first, last):
            index = col[:, k : k + 1]
            here = pl.ds(k * rows, rows)
            oh[here, :] = hot(index, (rows, table_rows), 1)
            mask[here, :] = jnp.where(
                jnp.broadcast_to(index, (rows, 128)) < table_rows, 1.0, 0.0
            ).astype(F32)

    front_hot(0, slots // 2)
    for copy in moving:
        copy.wait()

    moved = inner(arrive_hot, pool[...]).astype(BF16)
    out_snd[...] = inner(send_hot, moved).astype(BF16)
    lending = swap(
        out_snd,
        pl.ds(0, halo),
        pl.ds(rows + halo, halo),
        pl.ds(halo, halo),
        pl.ds(rows, halo),
        table,
        1,
    )
    table[pl.ds(0, rows)] = moved
    centre[...] = dot(moved, w_send[...])
    neigh[pl.ds(0, rows)] = dot(moved, w_recv[...]).astype(BF16)
    d_hid = by_transpose(cot[...], w_out[...])
    node_own = dot(moved, w_self[...])
    front_hot(slots // 2, slots)
    for copy in lending:
        copy.wait()
    neigh[pl.ds(rows, 2 * halo)] = dot(table[pl.ds(rows, 2 * halo)], w_recv[...]).astype(BF16)

    agg[...] = jnp.zeros_like(agg)
    span = CH * rows

    def front(c, carry):
        here = pl.ds(pl.multiple_of(c * span, span), span)
        pre = dot(oh[here, :], neigh[...]) + jnp.concatenate([centre[...]] * CH, axis=0)
        sig = sigmoid(pre)
        act = pre * sig
        low = act.astype(BF16)
        hid[here, :] = low
        ds1[here, :] = sig + act * (1.0 - sig)
        pre2 = dot(low, w_msg[...])
        sig2 = sigmoid(pre2)
        act2 = pre2 * sig2
        live = mask[here, :]
        md[here, :] = live * (sig2 + act2 * (1.0 - sig2))
        part = live * act2
        total = part[0:rows]
        for u in range(1, CH):
            total = total + part[u * rows : (u + 1) * rows]
        agg[...] += total
        return carry

    lax.fori_loop(0, slots // CH, front, 0)

    moved = table[pl.ds(0, rows)]
    agg_b = agg[...].astype(BF16)
    node_pre = node_own + dot(agg_b, w_agg[...])
    sig = sigmoid(node_pre)
    act = node_pre * sig
    node_hid = act.astype(BF16)
    updated_ref[...] = (moved.astype(F32) + dot(node_hid, w_out[...])).astype(BF16)
    d_node_pre = (d_hid * (sig + act * (1.0 - sig))).astype(BF16)
    d_agg[...] = by_transpose(d_node_pre, w_agg[...])
    g_out = inner(node_hid, cot[...])
    g_self = inner(moved, d_node_pre)
    g_agg = inner(agg_b, d_node_pre)
    d_local = cot[...].astype(F32) + by_transpose(d_node_pre, w_self[...])

    d_centre[...] = jnp.zeros_like(d_centre)
    d_neigh[...] = jnp.zeros_like(d_neigh)
    g_msg[...] = jnp.zeros_like(g_msg)

    def back(c, carry):
        here = pl.ds(pl.multiple_of(c * span, span), span)
        for u in range(CH):
            index = row[pl.ds(c * CH + u, 1), :]
            oht[:, u * rows : (u + 1) * rows] = hot(index, (table_rows, rows), 0)
        d_pre2 = (jnp.concatenate([d_agg[...]] * CH, axis=0) * md[here, :]).astype(BF16)
        d_pre = by_transpose(d_pre2, w_msg[...]) * ds1[here, :]
        g_msg[...] += inner(hid[here, :], d_pre2)
        total = d_pre[0:rows]
        for u in range(1, CH):
            total = total + d_pre[u * rows : (u + 1) * rows]
        d_centre[...] += total
        d_neigh[...] += dot(oht[...], d_pre.astype(BF16))
        return carry

    lax.fori_loop(0, slots // CH, back, 0)

    d_neigh_b = d_neigh[...].astype(BF16)
    ret_snd[...] = by_transpose(d_neigh_b[rows:], w_recv[...]).astype(BF16)
    returning = swap(
        ret_snd, pl.ds(0, halo), pl.ds(halo, halo), pl.ds(halo, halo), pl.ds(0, halo), ret_rcv, 2
    )
    d_centre_b = d_centre[...].astype(BF16)
    moved = table[pl.ds(0, rows)]
    g_send = inner(moved, d_centre_b)
    g_recv = inner(table[...], d_neigh_b)
    reduce = Sum(n_grp, n_y, n_z, 6, 0, reduce_scratch)
    reduce.share([g_send, g_recv, g_msg[...], g_self, g_agg, g_out])
    d_local = d_local + by_transpose(d_centre_b, w_send[...])
    d_local = d_local + by_transpose(d_neigh_b[0:rows], w_recv[...])
    reduce.line()
    for copy in returning:
        copy.wait()
    d_local = d_local + dot(send_hot, ret_rcv[...])
    grad_ref[...] = d_local.astype(BF16)
    reduce.spread()
    reduce.finish(steps_ref, 0)


def shards(n_grp, n_y, n_z, *args):
    nodes, leave_list, arrive_list, send_list, neighbours, valid = args[:6]
    weights, cotangent = args[6:12], args[12]
    operands = (
        nodes[0],
        leave_list,
        arrive_list,
        send_list,
        neighbours[0],
        valid[0],
        *weights,
        cotangent[0],
    )
    rows, width = operands[0].shape
    slots = operands[4].shape[1]
    migr, halo = leave_list.shape[1] // 2, send_list.shape[1] // 2
    table_rows = rows + 2 * halo
    edges = rows * slots
    plane = n_grp * n_y
    scratch = [pltpu.VMEM(x.shape, x.dtype) for x in operands]
    scratch += [
        pltpu.SemaphoreType.DMA((N_IN,)),
        pltpu.SemaphoreType.DMA((12,)),
        pltpu.VMEM((rows + 2 * migr, width), BF16),
        pltpu.VMEM((2 * migr, width), BF16),
        pltpu.VMEM((2 * halo, width), BF16),
        pltpu.VMEM((table_rows, width), BF16),
        pltpu.VMEM((2 * halo, width), BF16),
        pltpu.VMEM((2 * halo, width), BF16),
        pltpu.VMEM((rows, 128), jnp.int32),
        pltpu.VMEM((slots, rows), jnp.int32),
        pltpu.VMEM((edges, table_rows), BF16),
        pltpu.VMEM((table_rows, CH * rows), BF16),
        pltpu.VMEM((edges, width), F32),
        pltpu.VMEM((table_rows, width), BF16),
        pltpu.VMEM((rows, width), F32),
        pltpu.VMEM((rows, width), F32),
        pltpu.VMEM((edges, width), BF16),
        pltpu.VMEM((edges, width), F32),
        pltpu.VMEM((edges, width), F32),
        pltpu.VMEM((rows, width), F32),
        pltpu.VMEM((rows, width), F32),
        pltpu.VMEM((table_rows, width), F32),
        pltpu.VMEM((width, width), F32),
    ]
    scratch += sum_scratch(plane, n_z, 6)
    updated, grad_nodes, weight_steps = pl.pallas_call(
        functools.partial(kernel, n_grp, n_y, n_z, (rows, slots, migr, halo)),
        out_shape=(
            jax.ShapeDtypeStruct((rows, width), BF16),
            jax.ShapeDtypeStruct((rows, width), BF16),
            jax.ShapeDtypeStruct((6, width, width), F32),
        ),
        in_specs=[pl.BlockSpec(memory_space=pl.ANY)] * N_IN,
        out_specs=[pl.BlockSpec(memory_space=pltpu.VMEM)] * 3,
        scratch_shapes=scratch,
        compiler_params=pltpu.CompilerParams(
            collective_id=0, has_side_effects=True, vmem_limit_bytes=48 * 1024 * 1024
        ),
        name="particle_step",
    )(*operands)
    return (updated[None], grad_nodes[None], weight_steps)


def solution(mesh):
    n_grp, n_slab = mesh.shape["grp"], mesh.shape["slab"]
    n_z = 16 if n_slab > 16 else n_slab // 2
    in_specs = (
        P("grp", "slab", None),
        P("grp", "slab"),
        P("grp", "slab"),
        P("grp", "slab"),
        P("grp", "slab", None),
        P("grp", "slab", None),
        P(),
        P(),
        P(),
        P(),
        P(),
        P(),
        P("grp", "slab", None),
    )
    out_specs = (P("grp", "slab", None), P("grp", "slab", None), P())
    return jax.shard_map(
        functools.partial(shards, n_grp, n_slab // n_z, n_z),
        mesh=mesh,
        in_specs=in_specs,
        out_specs=out_specs,
        check_vma=False,
    )
```

time: 658 us -> 62.3 us (0.09)
  waiting for transfers between devices: 449 us -> 0 us
  local copies, waits for them, and re-layouts: 71.9 us -> 4.42 us
  other arithmetic: 57.9 us -> 0 us
  Pallas kernels: 0 us -> 56.8 us
  starting transfers between devices: 33.8 us -> 0 us
  matrix products: 27.3 us -> 0 us
  between operations: 14.4 us -> 0.8 us
    psum x1 -> x0, waiting for transfers between devices: 447 us -> none  [shards(): total = lax.psum(grads, ('grp', 'slab'))]
    pallas_call x0 -> x1, Pallas kernels: none -> 56.8 us  [shards(): pl.pallas_call(functools.partial(kernel, n_grp, n_y, n_z, (rows, slots, m...]
    gather x11 -> x0, local copies, waits for them, and re-layouts: 52.4 us -> none  [the longest x8 49.4 us: edge_front(): jnp.take(neigh, nbr_blk.reshape(-1), axis=0).reshape(block, slots, width)]
    scatter-add x6 -> x0, other arithmetic: 48.3 us -> none  [the longest x4 46.3 us: edge_back(): jax.ops.segment_sum(d_pre.reshape(-1, width), nbr_blk.reshape(-1), num_se...]
    ppermute x6 -> x0, starting transfers between devices: 33.8 us -> none  [the longest x3 25.6 us: with_halo(): after = lax.ppermute(first, axis, down)]
    dot_general x32 -> x0, matrix products: 27.3 us -> none  [the longest x8 10.3 us: edge_front(): jnp.dot(hid, w_msg, preferred_element_type=jnp.float32)]
  transfers between devices with their start and end apart: 7 -> 0, of which waited for: 3 -> 0; matrix products, arithmetic and copies ran while one was open for 1% -> 0% of each run, Pallas kernels for 0% -> 0%
where the time goes in v1:
time: 62.3 us; the launch traced here: 62 us
  Pallas kernels  56.8 us (91%)
  local copies, waits for them, and re-layouts  4.42 us (7%)
  between operations  0.8 us (1%)
    pallas_call x1, Pallas kernels, shards(): pl.pallas_call(functools.partial(kernel, n_grp, n_y, n_z, (rows, slots, m...  56.8 us
    unnamed x27, local copies, waits for them, and re-layouts  4.42 us

profile of v1, /device:TPU:1, one launch (start us, length us, event | category | flops | bytes accessed | tf_op | source)
XLA Modules:
  0.0 62.0 jit_solution(13898201862699493423)
XLA Ops:
  0.6 0.0 copy-start.3
  0.6 0.0 copy-start.4
  0.7 0.0 copy-start.5
  0.7 0.0 copy-start.6
  0.7 0.0 copy-start.7
  0.7 0.0 copy-start.10
  0.7 0.9 %copy.16 = s32[1,256,32]{2,1,0:T(8,128)S(1)} copy(s32[1,256,32]{1,2,0:T(8,128)} %param.17) | data formatting | bytes 65536 | tf_op args[4]
  1.6 0.0 copy-start
  1.6 0.0 copy-start.1
  1.6 0.0 copy-start.2
  1.6 0.9 %copy.17 = s32[1,256,32]{2,1,0:T(8,128)S(1)} copy(s32[1,256,32]{1,2,0:T(8,128)} %param.18) | data formatting | bytes 65536 | tf_op args[5]
  2.5 0.0 copy-start.8
  2.5 0.0 copy-start.9
  2.5 0.0 copy-done.3
  2.6 0.0 copy-done.4
  2.6 0.0 copy-done.5
  2.6 0.0 copy-done.6
  2.6 0.0 copy-done.7
  2.6 0.0 copy-done.10
  2.6 0.6 copy-done.8
  3.2 56.8 %particle_step.1 = (bf16[256,128]{1,0:T(8,128)(2,1)S(1)}, bf16[256,128]{1,0:T(8,128)(2,1)S(1)}, f32[6,128,128]{2,1,0:T(8,128)S(1)}) custom-call(bf16[256,128]{1,0:T(8,128)(2,1)S(1)} %bitcast.8, s32[1,64]{1,0:T(1,128)S(1)} %copy-done.9, s32[1,256]{1,0:T(1,128)S(1)} %copy-done.8, s32[1,128]{1,0:T(1,128)S(1)} %copy-done.10, s32[256,32]{1,0:T(8,128)S(1)} %bitcast.6, ...), custom_call_target="tpu_custom_call" | custom-call | tf_op jit(solution)/shard_map/particle_step/pallas_call | solution.py:458
  60.0 0.6 %copy.21 = bf16[1,256,128]{2,1,0:T(8,128)(2,1)} copy(bf16[1,256,128]{2,1,0:T(8,128)(2,1)S(1)} %bitcast.11) | data formatting | bytes 131072
  60.7 0.6 %copy.22 = bf16[1,256,128]{2,1,0:T(8,128)(2,1)} copy(bf16[1,256,128]{2,1,0:T(8,128)(2,1)S(1)} %bitcast.10) | data formatting | bytes 131072
  61.3 0.7 %copy.23 = f32[6,128,128]{2,1,0:T(8,128)} copy(f32[6,128,128]{2,1,0:T(8,128)S(1)} %get-tuple-element.14) | data formatting | bytes 786432
  (4 shorter events, 0.0 us)
Async XLA Ops:
  0.6 1.9 %copy-start.3 = (bf16[128,128]{1,0:T(8,128)(2,1)S(1)}, bf16[128,128]{1,0:T(8,128)(2,1)}, u32[]{:S(2)}) copy-start(bf16[128,128]{1,0:T(8,128)(2,1)} %refs_7_.1) | copy-start | bytes 98308
  0.6 1.9 %copy-start.4 = (bf16[128,128]{1,0:T(8,128)(2,1)S(1)}, bf16[128,128]{1,0:T(8,128)(2,1)}, u32[]{:S(2)}) copy-start(bf16[128,128]{1,0:T(8,128)(2,1)} %refs_8_.1) | copy-start | bytes 98308
  0.7 1.9 %copy-start.5 = (bf16[128,128]{1,0:T(8,128)(2,1)S(1)}, bf16[128,128]{1,0:T(8,128)(2,1)}, u32[]{:S(2)}) copy-start(bf16[128,128]{1,0:T(8,128)(2,1)} %refs_9_.1) | copy-start | bytes 98308
  0.7 1.9 %copy-start.6 = (bf16[128,128]{1,0:T(8,128)(2,1)S(1)}, bf16[128,128]{1,0:T(8,128)(2,1)}, u32[]{:S(2)}) copy-start(bf16[128,128]{1,0:T(8,128)(2,1)} %refs_10_.1) | copy-start | bytes 98308
  0.7 1.9 %copy-start.7 = (bf16[128,128]{1,0:T(8,128)(2,1)S(1)}, bf16[128,128]{1,0:T(8,128)(2,1)}, u32[]{:S(2)}) copy-start(bf16[128,128]{1,0:T(8,128)(2,1)} %refs_11_.1) | copy-start | bytes 98308
  0.7 1.9 %copy-start.10 = (s32[1,128]{1,0:T(1,128)S(1)}, s32[1,128]{1,0:T(1,128)}, u32[]{:S(2)}) copy-start(s32[1,128]{1,0:T(1,128)} %refs_3_.1) | copy-start | bytes 1540
  1.6 1.0 %copy-start = (bf16[1,256,128]{2,1,0:T(8,128)(2,1)S(1)}, bf16[1,256,128]{2,1,0:T(8,128)(2,1)}, u32[]{:S(2)}) copy-start(bf16[1,256,128]{2,1,0:T(8,128)(2,1)} %param.13) | copy-start | bytes 196612
  1.6 1.0 %copy-start.1 = (bf16[1,256,128]{2,1,0:T(8,128)(2,1)S(1)}, bf16[1,256,128]{2,1,0:T(8,128)(2,1)}, u32[]{:S(2)}) copy-start(bf16[1,256,128]{2,1,0:T(8,128)(2,1)} %param.25) | copy-start | bytes 196612
  1.6 1.0 %copy-start.2 = (bf16[128,128]{1,0:T(8,128)(2,1)S(1)}, bf16[128,128]{1,0:T(8,128)(2,1)}, u32[]{:S(2)}) copy-start(bf16[128,128]{1,0:T(8,128)(2,1)} %refs_6_.1) | copy-start | bytes 98308
  2.5 0.7 %copy-start.8 = (s32[1,256]{1,0:T(1,128)S(1)}, s32[1,256]{1,0:T(1,128)}, u32[]{:S(2)}) copy-start(s32[1,256]{1,0:T(1,128)} %refs_2_.1) | copy-start | bytes 3076
  2.5 0.7 %copy-start.9 = (s32[1,64]{1,0:T(1,128)S(1)}, s32[1,64]{1,0:T(1,128)}, u32[]{:S(2)}) copy-start(s32[1,64]{1,0:T(1,128)} %refs_1_.1) | copy-start | bytes 772

commit v2 on v1

--- a/solution.py
+++ b/solution.py
@@ -12,8 +12,10 @@
 BF16 = jnp.bfloat16
 
 
-def sigmoid(value):
-    return 0.5 * jnp.tanh(0.5 * value) + 0.5
+def silu_pair(half):
+    up = 1.0 + jnp.tanh(half)
+    act = half * up
+    return act, up * (1.0 + (half + half) - act)
 
 
 def dot(left, right):
@@ -26,6 +28,10 @@
 
 def by_transpose(left, right):
     return lax.dot_general(left, right, (((1,), (1,)), ((), ())), preferred_element_type=F32)
+
+
+def half(weights):
+    return (0.5 * weights.astype(F32)).astype(BF16)
 
 
 def hot(index, shape, dim):
@@ -181,7 +187,7 @@
 
 
 N_IN = 13
-CH = 4
+CH = 16
 
 
 def kernel(n_grp, n_y, n_z, dims, *refs):
@@ -194,13 +200,12 @@
     (
         in_sems,
         halo_sems,
-        pool,
-        mig_snd,
-        out_snd,
+        snd,
+        rcv,
+        far_rows,
         table,
         ret_snd,
         ret_rcv,
-        col,
         row,
         oh,
         oht,
@@ -215,8 +220,8 @@
         d_centre,
         d_neigh,
         g_msg,
-    ) = scratch[N_IN : N_IN + 23]
-    reduce_scratch = scratch[N_IN + 23 :]
+    ) = scratch[N_IN : N_IN + 22]
+    reduce_scratch = scratch[N_IN + 22 :]
     (nodes, leave, arrive, send, nbr, valid, w_send, w_recv, w_msg, w_self, w_agg, w_out, cot) = held
 
     g, slab = lax.axis_index("grp"), lax.axis_index("slab")
@@ -226,13 +231,15 @@
     q = g * n_y + y
     lower = (g, lax.rem(slab + n_slab - 1, n_slab))
     upper = (g, lax.rem(slab + 1, n_slab))
+    lower2 = (g, lax.rem(slab + n_slab - 2, n_slab))
+    upper2 = (g, lax.rem(slab + 2, n_slab))
 
     loads = [pltpu.make_async_copy(ins[i], held[i], in_sems.at[i]) for i in range(N_IN)]
     for i in range(N_IN):
         loads[i].start()
 
     barrier = pltpu.get_barrier_semaphore()
-    for to in (lower, upper):
+    for to in (lower, upper, lower2, upper2):
         pl.semaphore_signal(barrier, inc=1, device_id=to, device_id_type=MESH)
 
     def greet_plane(t, carry):
@@ -253,79 +260,67 @@
     lax.fori_loop(1, plane, greet_plane, 0)
     lax.fori_loop(1, n_z, greet_line, 0)
 
-    def swap(src, low_src, low_dst, up_src, up_dst, dst, stage):
-        size = low_src.size
-        copies = []
-        for k, (a, b, to) in enumerate(((low_src, low_dst, lower), (up_src, up_dst, upper))):
-            copies.append(
-                pltpu.make_async_remote_copy(
-                    src_ref=src.at[a],
-                    dst_ref=dst.at[b],
-                    send_sem=halo_sems.at[4 * stage + k],
-                    recv_sem=halo_sems.at[4 * stage + 2 + k],
-                    device_id=to,
-                    device_id_type=MESH,
-                )
-            )
-        for copy in copies:
-            copy.start()
-        return copies
-
-    loads[0].wait()
-    loads[1].wait()
-    mig_snd[...] = inner(hot(leave[...], (rows, 2 * migr), 0), nodes[...]).astype(BF16)
-    pl.semaphore_wait(barrier, plane + n_z)
-    moving = swap(
-        mig_snd,
-        pl.ds(0, migr),
-        pl.ds(rows + migr, migr),
-        pl.ds(migr, migr),
-        pl.ds(rows, migr),
-        pool,
-        0,
-    )
-    pool[pl.ds(0, rows)] = nodes[...]
-    for i in range(2, N_IN):
+    def send_to(src, dst, k, to):
+        return pltpu.make_async_remote_copy(
+            src_ref=src,
+            dst_ref=dst,
+            send_sem=halo_sems.at[2 * k],
+            recv_sem=halo_sems.at[2 * k + 1],
+            device_id=to,
+            device_id_type=MESH,
+        )
+
+    for i in range(4):
         loads[i].wait()
+    mine = nodes[...]
     arrive_hot = hot(arrive[...], (rows + 2 * migr, rows), 0)
     send_hot = hot(send[...], (rows, 2 * halo), 0)
-    marked = jnp.where(valid[...] > 0, nbr[...], table_rows)
-    col[:, pl.ds(0, slots)] = marked
-    row[...] = col[...].T[0:slots]
-
-    def front_hot(first, last):
-        for k in range(first, last):
-            index = col[:, k : k + 1]
-            here = pl.ds(k * rows, rows)
-            oh[here, :] = hot(index, (rows, table_rows), 1)
-            mask[here, :] = jnp.where(
-                jnp.broadcast_to(index, (rows, 128)) < table_rows, 1.0, 0.0
-            ).astype(F32)
-
-    front_hot(0, slots // 2)
-    for copy in moving:
+    moving = inner(hot(leave[...], (rows, 2 * migr), 0), mine).astype(BF16)
+    chosen = dot(arrive_hot, send_hot).astype(BF16)
+    lent = inner(chosen[0:rows], mine).astype(BF16)
+    picks = chosen[rows:]
+    down, up = moving[0:migr], moving[migr:]
+    for k, (part, leaving) in enumerate(((lent[0:halo], down), (lent[halo:], up))):
+        snd[k, 0:halo] = part
+        snd[k, halo : halo + 2 * migr] = picks
+        snd[k, halo + 2 * migr :] = leaving
+    pl.semaphore_wait(barrier, plane + n_z + 2)
+    fetching = []
+    for k, (near, far) in enumerate(((lower, lower2), (upper, upper2))):
+        fetching.append(send_to(snd.at[k], rcv.at[k], k, near))
+        fetching.append(
+            send_to(snd.at[k, pl.ds(halo + 2 * migr, migr)], far_rows.at[k], 2 + k, far)
+        )
+    for copy in fetching:
+        copy.start()
+    for i in range(4, N_IN):
+        loads[i].wait()
+    row[...] = jnp.where(valid[...] > 0, nbr[...], table_rows)
+    across = row[...].T
+    for k in range(slots):
+        index = across[:, k : k + 1]
+        here = pl.ds(k * rows, rows)
+        oh[here, :] = hot(index, (rows, table_rows), 1)
+        mask[here, :] = jnp.where(
+            jnp.broadcast_to(index, (rows, 128)) < table_rows, 1.0, 0.0
+        ).astype(F32)
+    d_hid = by_transpose(cot[...], w_out[...])
+    w_msg_half = half(w_msg[...])
+    kept = inner(arrive_hot[0:rows], mine)
+    for copy in fetching:
         copy.wait()
 
-    moved = inner(arrive_hot, pool[...]).astype(BF16)
-    out_snd[...] = inner(send_hot, moved).astype(BF16)
-    lending = swap(
-        out_snd,
-        pl.ds(0, halo),
-        pl.ds(rows + halo, halo),
-        pl.ds(halo, halo),
-        pl.ds(rows, halo),
-        table,
-        1,
-    )
+    from_below, from_above = rcv.at[1], rcv.at[0]
+    low_new, high_new = from_below[halo + 2 * migr :], from_above[halo + 2 * migr :]
+    moved = kept + inner(arrive_hot[rows:], jnp.concatenate([low_new, high_new], axis=0))
+    moved = moved.astype(BF16)
+    low_rows = inner(from_below[halo : halo + 2 * migr], jnp.concatenate([far_rows[1], down], axis=0))
+    high_rows = inner(from_above[halo : halo + 2 * migr], jnp.concatenate([up, far_rows[0]], axis=0))
     table[pl.ds(0, rows)] = moved
-    centre[...] = dot(moved, w_send[...])
-    neigh[pl.ds(0, rows)] = dot(moved, w_recv[...]).astype(BF16)
-    d_hid = by_transpose(cot[...], w_out[...])
-    node_own = dot(moved, w_self[...])
-    front_hot(slots // 2, slots)
-    for copy in lending:
-        copy.wait()
-    neigh[pl.ds(rows, 2 * halo)] = dot(table[pl.ds(rows, 2 * halo)], w_recv[...]).astype(BF16)
+    table[pl.ds(rows, halo)] = from_below[0:halo] + low_rows[halo:].astype(BF16)
+    table[pl.ds(rows + halo, halo)] = from_above[0:halo] + high_rows[0:halo].astype(BF16)
+    neigh[...] = (0.5 * dot(table[...], w_recv[...])).astype(BF16)
+    centre[...] = 0.5 * dot(moved, w_send[...])
 
     agg[...] = jnp.zeros_like(agg)
     span = CH * rows
@@ -333,17 +328,14 @@
     def front(c, carry):
         here = pl.ds(pl.multiple_of(c * span, span), span)
         pre = dot(oh[here, :], neigh[...]) + jnp.concatenate([centre[...]] * CH, axis=0)
-        sig = sigmoid(pre)
-        act = pre * sig
+        act, slope = silu_pair(pre)
         low = act.astype(BF16)
         hid[here, :] = low
-        ds1[here, :] = sig + act * (1.0 - sig)
-        pre2 = dot(low, w_msg[...])
-        sig2 = sigmoid(pre2)
-        act2 = pre2 * sig2
+        ds1[here, :] = slope
+        act, slope = silu_pair(dot(low, w_msg_half))
         live = mask[here, :]
-        md[here, :] = live * (sig2 + act2 * (1.0 - sig2))
-        part = live * act2
+        md[here, :] = live * slope
+        part = live * act
         total = part[0:rows]
         for u in range(1, CH):
             total = total + part[u * rows : (u + 1) * rows]
@@ -354,13 +346,11 @@
 
     moved = table[pl.ds(0, rows)]
     agg_b = agg[...].astype(BF16)
-    node_pre = node_own + dot(agg_b, w_agg[...])
-    sig = sigmoid(node_pre)
-    act = node_pre * sig
+    act, slope = silu_pair(0.5 * (dot(moved, w_self[...]) + dot(agg_b, w_agg[...])))
     node_hid = act.astype(BF16)
     updated_ref[...] = (moved.astype(F32) + dot(node_hid, w_out[...])).astype(BF16)
-    d_node_pre = (d_hid * (sig + act * (1.0 - sig))).astype(BF16)
-    d_agg[...] = by_transpose(d_node_pre, w_agg[...])
+    d_node_pre = (0.5 * d_hid * slope).astype(BF16)
+    d_agg[...] = 0.5 * by_transpose(d_node_pre, w_agg[...])
     g_out = inner(node_hid, cot[...])
     g_self = inner(moved, d_node_pre)
     g_agg = inner(agg_b, d_node_pre)
@@ -376,7 +366,7 @@
             index = row[pl.ds(c * CH + u, 1), :]
             oht[:, u * rows : (u + 1) * rows] = hot(index, (table_rows, rows), 0)
         d_pre2 = (jnp.concatenate([d_agg[...]] * CH, axis=0) * md[here, :]).astype(BF16)
-        d_pre = by_transpose(d_pre2, w_msg[...]) * ds1[here, :]
+        d_pre = by_transpose(d_pre2, w_msg_half) * ds1[here, :]
         g_msg[...] += inner(hid[here, :], d_pre2)
         total = d_pre[0:rows]
         for u in range(1, CH):
@@ -389,9 +379,12 @@
 
     d_neigh_b = d_neigh[...].astype(BF16)
     ret_snd[...] = by_transpose(d_neigh_b[rows:], w_recv[...]).astype(BF16)
-    returning = swap(
-        ret_snd, pl.ds(0, halo), pl.ds(halo, halo), pl.ds(halo, halo), pl.ds(0, halo), ret_rcv, 2
-    )
+    returning = [
+        send_to(ret_snd.at[pl.ds(0, halo)], ret_rcv.at[pl.ds(halo, halo)], 4, lower),
+        send_to(ret_snd.at[pl.ds(halo, halo)], ret_rcv.at[pl.ds(0, halo)], 5, upper),
+    ]
+    for copy in returning:
+        copy.start()
     d_centre_b = d_centre[...].astype(BF16)
     moved = table[pl.ds(0, rows)]
     g_send = inner(moved, d_centre_b)
@@ -417,13 +410,13 @@
         leave_list,
         arrive_list,
         send_list,
-        neighbours[0],
-        valid[0],
+        neighbours[0].T,
+        valid[0].T,
         *weights,
         cotangent[0],
     )
     rows, width = operands[0].shape
-    slots = operands[4].shape[1]
+    slots = operands[4].shape[0]
     migr, halo = leave_list.shape[1] // 2, send_list.shape[1] // 2
     table_rows = rows + 2 * halo
     edges = rows * slots
@@ -432,13 +425,12 @@
     scratch += [
         pltpu.SemaphoreType.DMA((N_IN,)),
         pltpu.SemaphoreType.DMA((12,)),
-        pltpu.VMEM((rows + 2 * migr, width), BF16),
-        pltpu.VMEM((2 * migr, width), BF16),
-        pltpu.VMEM((2 * halo, width), BF16),
+        pltpu.VMEM((2, halo + 3 * migr, width), BF16),
+        pltpu.VMEM((2, halo + 3 * migr, width), BF16),
+        pltpu.VMEM((2, migr, width), BF16),
         pltpu.VMEM((table_rows, width), BF16),
         pltpu.VMEM((2 * halo, width), BF16),
         pltpu.VMEM((2 * halo, width), BF16),
-        pltpu.VMEM((rows, 128), jnp.int32),
         pltpu.VMEM((slots, rows), jnp.int32),
         pltpu.VMEM((edges, table_rows), BF16),
         pltpu.VMEM((table_rows, CH * rows), BF16),
@@ -462,11 +454,11 @@
             jax.ShapeDtypeStruct((rows, width), BF16),
             jax.ShapeDtypeStruct((6, width, width), F32),
         ),
-        in_specs=[pl.BlockSpec(memory_space=pl.ANY)] * N_IN,
+        in_specs=[pl.BlockSpec(memory_space=pltpu.HBM)] * N_IN,
         out_specs=[pl.BlockSpec(memory_space=pltpu.VMEM)] * 3,
         scratch_shapes=scratch,
         compiler_params=pltpu.CompilerParams(
-            collective_id=0, has_side_effects=True, vmem_limit_bytes=48 * 1024 * 1024
+            collective_id=0, has_side_effects=True, vmem_limit_bytes=63 * 1024 * 1024
         ),
         name="particle_step",
     )(*operands)

time: 62.3 us -> 57.8 us (0.928)
  Pallas kernels: 56.8 us -> 53.1 us
    pallas_call x1, Pallas kernels: 56.8 us -> 53.1 us  [shards(): pl.pallas_call(functools.partial(kernel, n_grp, n_y, n_z, (rows, slots, m...]
    unnamed x27 -> x5, local copies, waits for them, and re-layouts: 4.42 us -> 3.9 us
where the time goes in v2:
time: 57.8 us; the launch traced here: 57.6 us
  Pallas kernels  53.1 us (92%)
  local copies, waits for them, and re-layouts  3.9 us (7%)
  between operations  0.65 us (1%)
    pallas_call x1, Pallas kernels, shards(): pl.pallas_call(functools.partial(kernel, n_grp, n_y, n_z, (rows, slots, m...  53.1 us
    unnamed x5, local copies, waits for them, and re-layouts  3.9 us

profile of v2, /device:TPU:1, one launch (start us, length us, event | category | flops | bytes accessed | tf_op | source)
XLA Modules:
  0.0 57.6 jit_solution(2926794405896088247)
XLA Ops:
  0.6 53.1 %particle_step.1 = (bf16[256,128]{1,0:T(8,128)(2,1)}, bf16[256,128]{1,0:T(8,128)(2,1)}, f32[6,128,128]{2,1,0:T(8,128)}) custom-call(bf16[256,128]{1,0:T(8,128)(2,1)} %bitcast.12, s32[1,64]{1,0:T(1,128)} %refs_1_.1, s32[1,256]{1,0:T(1,128)} %refs_2_.1, s32[1,128]{1,0:T(1,128)} %refs_3_.1, s32[32,256]{1,0:T(8,128)} %bitcast.14, s32[32,256]{1,0:T(8,128)} %bitcast.15, ...), custom_call_target="tpu_custom_call" | custom-call | tf_op jit(solution)/shard_map/particle_step/pallas_call | solution.py:450
  53.7 0.0 copy-start
  53.7 1.5 %copy.19 = bf16[1,256,128]{2,1,0:T(8,128)(2,1)} copy(bf16[1,256,128]{2,1,0:T(8,128)(2,1)} %bitcast.11) | data formatting | bytes 131072
  55.2 0.0 copy-done
  55.2 0.6 %copy.20 = bf16[1,256,128]{2,1,0:T(8,128)(2,1)} copy(bf16[1,256,128]{2,1,0:T(8,128)(2,1)S(1)} %bitcast.10) | data formatting | bytes 131072
  55.9 1.8 %copy.21 = f32[6,128,128]{2,1,0:T(8,128)} copy(f32[6,128,128]{2,1,0:T(8,128)} %get-tuple-element.14) | data formatting | bytes 786432
Async XLA Ops:
  53.7 1.5 %copy-start = (bf16[256,128]{1,0:T(8,128)(2,1)S(1)}, bf16[256,128]{1,0:T(8,128)(2,1)}, u32[]{:S(2)}) copy-start(bf16[256,128]{1,0:T(8,128)(2,1)} %get-tuple-element.7) | copy-start | bytes 196612

commit v3 on v2

--- a/solution.py
+++ b/solution.py
@@ -78,19 +78,24 @@
                 b = m * tiles + t
                 self.snd[b // self.per, b % self.per] = low[t * 16 : (t + 1) * 16]
 
-        def step(t, carry):
-            block = lax.rem(self.block + t, self.plane)
+        for slot, (dg, dy) in enumerate(self.far_first()):
+            to_g, to_y = lax.rem(self.g + dg, self.n_grp), lax.rem(self.y + dy, self.n_y)
+            to = to_g * self.n_y + to_y
+            block = lax.rem(to + self.plane - self.offset, self.plane)
 
             @pl.when(block < self.owners)
             def _():
-                to = lax.rem(block + self.offset, self.plane)
                 self.copy(
-                    self.snd.at[block], self.rcv.at[self.plane - 1 - t], 0, self.device(to, self.z)
+                    self.snd.at[block], self.rcv.at[slot], 0, (to_g, to_y * self.n_z + self.z)
                 ).start()
 
-            return carry
-
-        lax.fori_loop(1, self.plane, step, 0)
+    def far_first(self):
+        def hops(step):
+            chips = (step[0] + 1) // 2
+            return min(chips, self.n_grp // 2 - chips) + min(step[1], self.n_y - step[1])
+
+        places = [(dg, dy) for dg in range(self.n_grp) for dy in range(self.n_y) if dg or dy]
+        return sorted(places, key=hops, reverse=True)
 
     def line(self):
         @pl.when(self.is_owner)
@@ -102,21 +107,11 @@
                 total = total + self.rcv[i].astype(F32)
             self.part[0] = total.astype(BF16)
             self.zrcv[self.n_z - 1] = total.astype(BF16)
-            half = self.n_z // 2
-
-            def step(t, carry):
-                to = lax.rem(self.z + half + t, self.n_z)
-                slot = lax.rem(self.n_z - 1 - half - t + self.n_z, self.n_z)
-
-                @pl.when(to != self.z)
-                def _():
-                    self.copy(
-                        self.part.at[0], self.zrcv.at[slot], 1, self.device(self.q, to)
-                    ).start()
-
-                return carry
-
-            lax.fori_loop(0, self.n_z, step, 0)
+            for t in sorted(range(1, self.n_z), key=lambda t: -min(t, self.n_z - t)):
+                to = lax.rem(self.z + t, self.n_z)
+                self.copy(
+                    self.part.at[0], self.zrcv.at[self.n_z - 1 - t], 1, self.device(self.q, to)
+                ).start()
 
     def spread(self):
         @pl.when(self.is_owner)
@@ -128,14 +123,12 @@
             self.part[1] = total.astype(BF16)
             self.all[self.block] = total.astype(BF16)
 
-            def step(t, carry):
-                to = lax.rem(self.q + t, self.plane)
-                self.copy(
-                    self.part.at[1], self.all.at[self.block], 2, self.device(to, self.z)
-                ).start()
-                return carry
-
-            lax.fori_loop(1, self.plane, step, 0)
+            for dg, dy in self.far_first():
+                to = (
+                    lax.rem(self.g + dg, self.n_grp),
+                    lax.rem(self.y + dy, self.n_y) * self.n_z + self.z,
+                )
+                self.copy(self.part.at[1], self.all.at[self.block], 2, to).start()
 
     def slot_of(self, i):
         return lax.rem(self.n_z - 1 - (self.z - i) + 2 * self.n_z, self.n_z)
@@ -200,6 +193,9 @@
     (
         in_sems,
         halo_sems,
+        y_sem,
+        two_sem,
+        four_sem,
         snd,
         rcv,
         far_rows,
@@ -220,8 +216,8 @@
         d_centre,
         d_neigh,
         g_msg,
-    ) = scratch[N_IN : N_IN + 22]
-    reduce_scratch = scratch[N_IN + 22 :]
+    ) = scratch[N_IN : N_IN + 25]
+    reduce_scratch = scratch[N_IN + 25 :]
     (nodes, leave, arrive, send, nbr, valid, w_send, w_recv, w_msg, w_self, w_agg, w_out, cot) = held
 
     g, slab = lax.axis_index("grp"), lax.axis_index("slab")
@@ -238,27 +234,27 @@
     for i in range(N_IN):
         loads[i].start()
 
+    def along(dy, dz):
+        return (g, lax.rem(y + dy, n_y) * n_z + lax.rem(z + dz, n_z))
+
+    def steps(distances, size):
+        return sorted({d % size for d in distances} - {0})
+
+    near = [lower, upper, lower2, upper2]
+    near += [(lax.rem(g + d, n_grp), slab) for d in range(1, n_grp)]
+    near += [along(d, 0) for d in range(1, n_y)]
+    near += [along(0, d) for d in steps((1, -1, 2, -2), n_z)]
     barrier = pltpu.get_barrier_semaphore()
-    for to in (lower, upper, lower2, upper2):
+    for to in near:
         pl.semaphore_signal(barrier, inc=1, device_id=to, device_id_type=MESH)
 
-    def greet_plane(t, carry):
-        to = lax.rem(q + t, plane)
-        pl.semaphore_signal(
-            barrier,
-            inc=1,
-            device_id=(to // n_y, lax.rem(to, n_y) * n_z + z),
-            device_id_type=MESH,
-        )
-        return carry
-
-    def greet_line(t, carry):
-        to = (g, y * n_z + lax.rem(z + t, n_z))
-        pl.semaphore_signal(barrier, inc=1, device_id=to, device_id_type=MESH)
-        return carry
-
-    lax.fori_loop(1, plane, greet_plane, 0)
-    lax.fori_loop(1, n_z, greet_line, 0)
+    def pass_on(sem, targets):
+        for to in targets:
+            pl.semaphore_signal(sem, inc=1, device_id=to, device_id_type=MESH)
+
+    over_y = [along(d, 0) for d in range(1, n_y)]
+    two_on = [along(0, d) for d in steps((2, -2), n_z)]
+    four_on = [along(0, d) for d in steps((4, -4), n_z)]
 
     def send_to(src, dst, k, to):
         return pltpu.make_async_remote_copy(
@@ -284,7 +280,7 @@
         snd[k, 0:halo] = part
         snd[k, halo : halo + 2 * migr] = picks
         snd[k, halo + 2 * migr :] = leaving
-    pl.semaphore_wait(barrier, plane + n_z + 2)
+    pl.semaphore_wait(barrier, len(near))
     fetching = []
     for k, (near, far) in enumerate(((lower, lower2), (upper, upper2))):
         fetching.append(send_to(snd.at[k], rcv.at[k], k, near))
@@ -293,6 +289,8 @@
         )
     for copy in fetching:
         copy.start()
+    pass_on(y_sem, over_y)
+    pass_on(two_sem, two_on)
     for i in range(4, N_IN):
         loads[i].wait()
     row[...] = jnp.where(valid[...] > 0, nbr[...], table_rows)
@@ -344,6 +342,10 @@
 
     lax.fori_loop(0, slots // CH, front, 0)
 
+    if two_on:
+        pl.semaphore_wait(two_sem, len(two_on))
+    pass_on(four_sem, four_on)
+
     moved = table[pl.ds(0, rows)]
     agg_b = agg[...].astype(BF16)
     act, slope = silu_pair(0.5 * (dot(moved, w_self[...]) + dot(agg_b, w_agg[...])))
@@ -389,10 +391,14 @@
     moved = table[pl.ds(0, rows)]
     g_send = inner(moved, d_centre_b)
     g_recv = inner(table[...], d_neigh_b)
+    if over_y:
+        pl.semaphore_wait(y_sem, len(over_y))
     reduce = Sum(n_grp, n_y, n_z, 6, 0, reduce_scratch)
     reduce.share([g_send, g_recv, g_msg[...], g_self, g_agg, g_out])
     d_local = d_local + by_transpose(d_centre_b, w_send[...])
     d_local = d_local + by_transpose(d_neigh_b[0:rows], w_recv[...])
+    if four_on:
+        pl.semaphore_wait(four_sem, len(four_on))
     reduce.line()
     for copy in returning:
         copy.wait()
@@ -415,6 +421,7 @@
         *weights,
         cotangent[0],
     )
+    operands = [pltpu.with_memory_space_constraint(x, pltpu.HBM) for x in operands]
     rows, width = operands[0].shape
     slots = operands[4].shape[0]
     migr, halo = leave_list.shape[1] // 2, send_list.shape[1] // 2
@@ -425,6 +432,9 @@
     scratch += [
         pltpu.SemaphoreType.DMA((N_IN,)),
         pltpu.SemaphoreType.DMA((12,)),
+        pltpu.SemaphoreType.REGULAR,
+        pltpu.SemaphoreType.REGULAR,
+        pltpu.SemaphoreType.REGULAR,
         pltpu.VMEM((2, halo + 3 * migr, width), BF16),
         pltpu.VMEM((2, halo + 3 * migr, width), BF16),
         pltpu.VMEM((2, migr, width), BF16),
@@ -458,7 +468,7 @@
         out_specs=[pl.BlockSpec(memory_space=pltpu.VMEM)] * 3,
         scratch_shapes=scratch,
         compiler_params=pltpu.CompilerParams(
-            collective_id=0, has_side_effects=True, vmem_limit_bytes=63 * 1024 * 1024
+            collective_id=0, has_side_effects=True, vmem_limit_bytes=52 * 1024 * 1024
         ),
         name="particle_step",
     )(*operands)

time: 57.8 us -> 50.2 us (0.87)
  Pallas kernels: 53.1 us -> 47.3 us
  local copies, waits for them, and re-layouts: 3.9 us -> 2.01 us
    pallas_call x1, Pallas kernels: 53.1 us -> 47.3 us  [shards(): pl.pallas_call(functools.partial(kernel, n_grp, n_y, n_z, (rows, slots, m...]
    unnamed x5 -> x3, local copies, waits for them, and re-layouts: 3.9 us -> 2.01 us
where the time goes in v3:
time: 50.2 us; the launch traced here: 50 us
  Pallas kernels  47.3 us (94%)
  local copies, waits for them, and re-layouts  2.01 us (4%)
  between operations  0.64 us (1%)
    pallas_call x1, Pallas kernels, shards(): pl.pallas_call(functools.partial(kernel, n_grp, n_y, n_z, (rows, slots, m...  47.3 us
    unnamed x3, local copies, waits for them, and re-layouts  2.01 us

profile of v3, /device:TPU:1, one launch (start us, length us, event | category | flops | bytes accessed | tf_op | source)
XLA Modules:
  0.0 50.0 jit_solution(15922122412637843220)
XLA Ops:
  0.6 47.3 %particle_step.1 = (bf16[256,128]{1,0:T(8,128)(2,1)S(1)}, bf16[256,128]{1,0:T(8,128)(2,1)S(1)}, f32[6,128,128]{2,1,0:T(8,128)S(1)}) custom-call(bf16[256,128]{1,0:T(8,128)(2,1)} %bitcast.12, s32[1,64]{1,0:T(1,128)} %refs_1_.1, s32[1,256]{1,0:T(1,128)} %refs_2_.1, s32[1,128]{1,0:T(1,128)} %refs_3_.1, s32[32,256]{1,0:T(8,128)} %bitcast.14, ...), custom_call_target="tpu_custom_call" | custom-call | tf_op jit(solution)/shard_map/particle_step/pallas_call | solution.py:460
  48.0 0.6 %copy.19 = bf16[1,256,128]{2,1,0:T(8,128)(2,1)} copy(bf16[1,256,128]{2,1,0:T(8,128)(2,1)S(1)} %bitcast.11) | data formatting | bytes 131072
  48.6 0.6 %copy.20 = bf16[1,256,128]{2,1,0:T(8,128)(2,1)} copy(bf16[1,256,128]{2,1,0:T(8,128)(2,1)S(1)} %bitcast.10) | data formatting | bytes 131072
  49.2 0.7 %copy.21 = f32[6,128,128]{2,1,0:T(8,128)} copy(f32[6,128,128]{2,1,0:T(8,128)S(1)} %get-tuple-element.14) | data formatting | bytes 786432

commit v4 on v3

--- a/solution.py
+++ b/solution.py
@@ -44,17 +44,18 @@
 
 
 class Sum:
-    def __init__(self, n_grp, n_y, n_z, mats, offset, scratch):
+    def __init__(self, n_grp, n_y, n_z, mats, from_end, scratch):
         self.n_grp, self.n_y, self.n_z = n_grp, n_y, n_z
-        self.mats, self.offset = mats, offset
+        self.mats = mats
         self.plane = n_grp * n_y
         self.per, self.owners = shares(self.plane, mats)
+        self.offset = self.plane - self.owners if from_end else 0
         self.snd, self.rcv, self.part, self.zrcv, self.all, self.sems = scratch
         self.g = lax.axis_index("grp")
         slab = lax.axis_index("slab")
         self.y, self.z = slab // n_z, lax.rem(slab, n_z)
         self.q = self.g * n_y + self.y
-        self.block = lax.rem(self.q + self.plane - offset, self.plane)
+        self.block = lax.rem(self.q + self.plane - self.offset, self.plane)
         self.is_owner = self.block < self.owners
 
     def device(self, q, z):
@@ -187,8 +188,9 @@
     rows, slots, migr, halo = dims
     table_rows = rows + 2 * halo
     ins = refs[:N_IN]
-    updated_ref, grad_ref, steps_ref = refs[N_IN : N_IN + 3]
-    scratch = refs[N_IN + 3 :]
+    both_ref, steps_ref = refs[N_IN : N_IN + 2]
+    updated_ref, grad_ref = both_ref.at[0], both_ref.at[1]
+    scratch = refs[N_IN + 2 :]
     held = scratch[:N_IN]
     (
         in_sems,
@@ -231,9 +233,6 @@
     upper2 = (g, lax.rem(slab + 2, n_slab))
 
     loads = [pltpu.make_async_copy(ins[i], held[i], in_sems.at[i]) for i in range(N_IN)]
-    for i in range(N_IN):
-        loads[i].start()
-
     def along(dy, dz):
         return (g, lax.rem(y + dy, n_y) * n_z + lax.rem(z + dz, n_z))
 
@@ -245,8 +244,13 @@
     near += [along(d, 0) for d in range(1, n_y)]
     near += [along(0, d) for d in steps((1, -1, 2, -2), n_z)]
     barrier = pltpu.get_barrier_semaphore()
-    for to in near:
+    for i, to in enumerate(near):
+        if i == 4:
+            for load in loads[:4]:
+                load.start()
         pl.semaphore_signal(barrier, inc=1, device_id=to, device_id_type=MESH)
+    for load in loads[4:]:
+        load.start()
 
     def pass_on(sem, targets):
         for to in targets:
@@ -302,6 +306,10 @@
         mask[here, :] = jnp.where(
             jnp.broadcast_to(index, (rows, 128)) < table_rows, 1.0, 0.0
         ).astype(F32)
+    for k in range(slots):
+        oht[k // CH, :, k % CH * rows : (k % CH + 1) * rows] = hot(
+            row[k : k + 1, :], (table_rows, rows), 0
+        )
     d_hid = by_transpose(cot[...], w_out[...])
     w_msg_half = half(w_msg[...])
     kept = inner(arrive_hot[0:rows], mine)
@@ -356,6 +364,11 @@
     g_out = inner(node_hid, cot[...])
     g_self = inner(moved, d_node_pre)
     g_agg = inner(agg_b, d_node_pre)
+    if over_y:
+        pl.semaphore_wait(y_sem, len(over_y))
+    early = Sum(n_grp, n_y, n_z, 3, False, reduce_scratch[:6])
+    late = Sum(n_grp, n_y, n_z, 3, True, reduce_scratch[6:])
+    early.share([g_self, g_agg, g_out])
     d_local = cot[...].astype(F32) + by_transpose(d_node_pre, w_self[...])
 
     d_centre[...] = jnp.zeros_like(d_centre)
@@ -364,9 +377,6 @@
 
     def back(c, carry):
         here = pl.ds(pl.multiple_of(c * span, span), span)
-        for u in range(CH):
-            index = row[pl.ds(c * CH + u, 1), :]
-            oht[:, u * rows : (u + 1) * rows] = hot(index, (table_rows, rows), 0)
         d_pre2 = (jnp.concatenate([d_agg[...]] * CH, axis=0) * md[here, :]).astype(BF16)
         d_pre = by_transpose(d_pre2, w_msg_half) * ds1[here, :]
         g_msg[...] += inner(hid[here, :], d_pre2)
@@ -374,12 +384,17 @@
         for u in range(1, CH):
             total = total + d_pre[u * rows : (u + 1) * rows]
         d_centre[...] += total
-        d_neigh[...] += dot(oht[...], d_pre.astype(BF16))
+        d_neigh[...] += dot(oht[c], d_pre.astype(BF16))
         return carry
 
     lax.fori_loop(0, slots // CH, back, 0)
 
     d_neigh_b = d_neigh[...].astype(BF16)
+    d_centre_b = d_centre[...].astype(BF16)
+    moved = table[pl.ds(0, rows)]
+    g_recv = inner(table[...], d_neigh_b)
+    g_send = inner(moved, d_centre_b)
+    late.share([g_send, g_recv, g_msg[...]])
     ret_snd[...] = by_transpose(d_neigh_b[rows:], w_recv[...]).astype(BF16)
     returning = [
         send_to(ret_snd.at[pl.ds(0, halo)], ret_rcv.at[pl.ds(halo, halo)], 4, lower),
@@ -387,25 +402,20 @@
     ]
     for copy in returning:
         copy.start()
-    d_centre_b = d_centre[...].astype(BF16)
-    moved = table[pl.ds(0, rows)]
-    g_send = inner(moved, d_centre_b)
-    g_recv = inner(table[...], d_neigh_b)
-    if over_y:
-        pl.semaphore_wait(y_sem, len(over_y))
-    reduce = Sum(n_grp, n_y, n_z, 6, 0, reduce_scratch)
-    reduce.share([g_send, g_recv, g_msg[...], g_self, g_agg, g_out])
+    if four_on:
+        pl.semaphore_wait(four_sem, len(four_on))
+    early.line()
     d_local = d_local + by_transpose(d_centre_b, w_send[...])
     d_local = d_local + by_transpose(d_neigh_b[0:rows], w_recv[...])
-    if four_on:
-        pl.semaphore_wait(four_sem, len(four_on))
-    reduce.line()
     for copy in returning:
         copy.wait()
     d_local = d_local + dot(send_hot, ret_rcv[...])
     grad_ref[...] = d_local.astype(BF16)
-    reduce.spread()
-    reduce.finish(steps_ref, 0)
+    late.line()
+    early.spread()
+    late.spread()
+    early.finish(steps_ref, 3)
+    late.finish(steps_ref, 0)
 
 
 def shards(n_grp, n_y, n_z, *args):
@@ -443,7 +453,7 @@
         pltpu.VMEM((2 * halo, width), BF16),
         pltpu.VMEM((slots, rows), jnp.int32),
         pltpu.VMEM((edges, table_rows), BF16),
-        pltpu.VMEM((table_rows, CH * rows), BF16),
+        pltpu.VMEM((slots // CH, table_rows, CH * rows), BF16),
         pltpu.VMEM((edges, width), F32),
         pltpu.VMEM((table_rows, width), BF16),
         pltpu.VMEM((rows, width), F32),
@@ -456,23 +466,22 @@
         pltpu.VMEM((table_rows, width), F32),
         pltpu.VMEM((width, width), F32),
     ]
-    scratch += sum_scratch(plane, n_z, 6)
-    updated, grad_nodes, weight_steps = pl.pallas_call(
+    scratch += sum_scratch(plane, n_z, 3) + sum_scratch(plane, n_z, 3)
+    both, weight_steps = pl.pallas_call(
         functools.partial(kernel, n_grp, n_y, n_z, (rows, slots, migr, halo)),
         out_shape=(
-            jax.ShapeDtypeStruct((rows, width), BF16),
-            jax.ShapeDtypeStruct((rows, width), BF16),
+            jax.ShapeDtypeStruct((2, rows, width), BF16),
             jax.ShapeDtypeStruct((6, width, width), F32),
         ),
         in_specs=[pl.BlockSpec(memory_space=pltpu.HBM)] * N_IN,
-        out_specs=[pl.BlockSpec(memory_space=pltpu.VMEM)] * 3,
+        out_specs=[pl.BlockSpec(memory_space=pltpu.VMEM)] * 2,
         scratch_shapes=scratch,
         compiler_params=pltpu.CompilerParams(
             collective_id=0, has_side_effects=True, vmem_limit_bytes=52 * 1024 * 1024
         ),
         name="particle_step",
     )(*operands)
-    return (updated[None], grad_nodes[None], weight_steps)
+    return (both[0][None], both[1][None], weight_steps)
 
 
 def solution(mesh):

time: 50.2 us -> 47.2 us (0.940)
  Pallas kernels: 47.3 us -> 45 us
  local copies, waits for them, and re-layouts: 2.01 us -> 1.41 us
    pallas_call x1, Pallas kernels: 47.3 us -> 45 us  [shards(): pl.pallas_call(functools.partial(kernel, n_grp, n_y, n_z, (rows, slots, m...]
    unnamed x3 -> x1, local copies, waits for them, and re-layouts: 2.01 us -> 0.75 us
    slice x0 -> x1, local copies, waits for them, and re-layouts: none -> 0.66 us  [shards(): return (both[0][None], both[1][None], weight_steps)]
where the time goes in v4:
time: 47.2 us; the launch traced here: 47 us
  Pallas kernels  45 us (95%)
  local copies, waits for them, and re-layouts  1.41 us (3%)
  between operations  0.64 us (1%)
    pallas_call x1, Pallas kernels, shards(): pl.pallas_call(functools.partial(kernel, n_grp, n_y, n_z, (rows, slots, m...  45 us

profile of v4, /device:TPU:1, one launch (start us, length us, event | category | flops | bytes accessed | tf_op | source)
XLA Modules:
  0.0 47.0 jit_solution(8201403990448206497)
XLA Ops:
  0.6 45.0 %particle_step.1 = (bf16[2,256,128]{2,1,0:T(8,128)(2,1)S(1)}, f32[6,128,128]{2,1,0:T(8,128)S(1)}) custom-call(bf16[256,128]{1,0:T(8,128)(2,1)} %bitcast.8, s32[1,64]{1,0:T(1,128)} %refs_1_.1, s32[1,256]{1,0:T(1,128)} %refs_2_.1, s32[1,128]{1,0:T(1,128)} %refs_3_.1, s32[32,256]{1,0:T(8,128)} %bitcast.10, s32[32,256]{1,0:T(8,128)} %bitcast.11, ...), custom_call_target="tpu_custom_call" | custom-call | tf_op jit(solution)/shard_map/particle_step/pallas_call | solution.py:470
  45.6 0.7 %fusion = (bf16[1,256,128]{2,1,0:T(8,128)(2,1)}, bf16[1,256,128]{2,1,0:T(8,128)(2,1)}) fusion(bf16[2,256,128]{2,1,0:T(8,128)(2,1)S(1)} %get-tuple-element.5), kind=kLoop, calls=%fused_computation | loop fusion | bytes 262144 | tf_op jit(solution)/shard_map/slice | solution.py:484
  46.3 0.7 %copy.17 = f32[6,128,128]{2,1,0:T(8,128)} copy(f32[6,128,128]{2,1,0:T(8,128)S(1)} %get-tuple-element.14) | data formatting | bytes 786432

commit v5 on v4

--- a/solution.py
+++ b/solution.py
@@ -15,7 +15,7 @@
 def silu_pair(half):
     up = 1.0 + jnp.tanh(half)
     act = half * up
-    return act, up * (1.0 + (half + half) - act)
+    return act, up + act * (2.0 - up)
 
 
 def dot(left, right):
@@ -28,6 +28,27 @@
 
 def by_transpose(left, right):
     return lax.dot_general(left, right, (((1,), (1,)), ((), ())), preferred_element_type=F32)
+
+
+def twice(weights):
+    zero = jnp.zeros_like(weights)
+    return jnp.concatenate(
+        [
+            jnp.concatenate([weights, zero], axis=1),
+            jnp.concatenate([zero, weights], axis=1),
+        ],
+        axis=0,
+    )
+
+
+def beside(rows):
+    middle = rows.shape[0] // 2
+    return jnp.concatenate([rows[:middle], rows[middle:]], axis=1)
+
+
+def below(rows):
+    middle = rows.shape[1] // 2
+    return jnp.concatenate([rows[:, :middle], rows[:, middle:]], axis=0)
 
 
 def half(weights):
@@ -198,6 +219,9 @@
         y_sem,
         two_sem,
         four_sem,
+        w_pair,
+        w_half,
+        left,
         snd,
         rcv,
         far_rows,
@@ -218,8 +242,8 @@
         d_centre,
         d_neigh,
         g_msg,
-    ) = scratch[N_IN : N_IN + 25]
-    reduce_scratch = scratch[N_IN + 25 :]
+    ) = scratch[N_IN : N_IN + 28]
+    reduce_scratch = scratch[N_IN + 28 :]
     (nodes, leave, arrive, send, nbr, valid, w_send, w_recv, w_msg, w_self, w_agg, w_out, cot) = held
 
     g, slab = lax.axis_index("grp"), lax.axis_index("slab")
@@ -287,10 +311,10 @@
     pl.semaphore_wait(barrier, len(near))
     fetching = []
     for k, (near, far) in enumerate(((lower, lower2), (upper, upper2))):
-        fetching.append(send_to(snd.at[k], rcv.at[k], k, near))
         fetching.append(
             send_to(snd.at[k, pl.ds(halo + 2 * migr, migr)], far_rows.at[k], 2 + k, far)
         )
+        fetching.append(send_to(snd.at[k], rcv.at[k], k, near))
     for copy in fetching:
         copy.start()
     pass_on(y_sem, over_y)
@@ -299,19 +323,21 @@
         loads[i].wait()
     row[...] = jnp.where(valid[...] > 0, nbr[...], table_rows)
     across = row[...].T
+    middle = table_rows // 2
     for k in range(slots):
         index = across[:, k : k + 1]
         here = pl.ds(k * rows, rows)
         oh[here, :] = hot(index, (rows, table_rows), 1)
-        mask[here, :] = jnp.where(
-            jnp.broadcast_to(index, (rows, 128)) < table_rows, 1.0, 0.0
-        ).astype(F32)
+        index = jnp.broadcast_to(index, (rows, 128))
+        mask[here, :] = jnp.where(index < table_rows, 1.0, 0.0).astype(F32)
+        left[here, :] = jnp.where(index < middle, 1.0, 0.0).astype(BF16)
     for k in range(slots):
-        oht[k // CH, :, k % CH * rows : (k % CH + 1) * rows] = hot(
-            row[k : k + 1, :], (table_rows, rows), 0
-        )
+        index = row[k : k + 1, :]
+        index = jnp.where(index >= middle, index - middle, index)
+        oht[k // CH, :, k % CH * rows : (k % CH + 1) * rows] = hot(index, (middle, rows), 0)
     d_hid = by_transpose(cot[...], w_out[...])
-    w_msg_half = half(w_msg[...])
+    w_half[...] = half(w_msg[...])
+    w_pair[...] = twice(w_half[...])
     kept = inner(arrive_hot[0:rows], mine)
     for copy in fetching:
         copy.wait()
@@ -331,14 +357,14 @@
     agg[...] = jnp.zeros_like(agg)
     span = CH * rows
 
-    def front(c, carry):
-        here = pl.ds(pl.multiple_of(c * span, span), span)
+    def front(c):
+        here = pl.ds(c * span, span)
         pre = dot(oh[here, :], neigh[...]) + jnp.concatenate([centre[...]] * CH, axis=0)
         act, slope = silu_pair(pre)
         low = act.astype(BF16)
         hid[here, :] = low
         ds1[here, :] = slope
-        act, slope = silu_pair(dot(low, w_msg_half))
+        act, slope = silu_pair(below(dot(beside(low), w_pair[...])))
         live = mask[here, :]
         md[here, :] = live * slope
         part = live * act
@@ -346,9 +372,9 @@
         for u in range(1, CH):
             total = total + part[u * rows : (u + 1) * rows]
         agg[...] += total
-        return carry
-
-    lax.fori_loop(0, slots // CH, front, 0)
+
+    for c in range(slots // CH):
+        front(c)
 
     if two_on:
         pl.semaphore_wait(two_sem, len(two_on))
@@ -375,21 +401,24 @@
     d_neigh[...] = jnp.zeros_like(d_neigh)
     g_msg[...] = jnp.zeros_like(g_msg)
 
-    def back(c, carry):
-        here = pl.ds(pl.multiple_of(c * span, span), span)
+    def back(c):
+        here = pl.ds(c * span, span)
         d_pre2 = (jnp.concatenate([d_agg[...]] * CH, axis=0) * md[here, :]).astype(BF16)
-        d_pre = by_transpose(d_pre2, w_msg_half) * ds1[here, :]
+        d_pre = by_transpose(d_pre2, w_half[...]) * ds1[here, :]
         g_msg[...] += inner(hid[here, :], d_pre2)
         total = d_pre[0:rows]
         for u in range(1, CH):
             total = total + d_pre[u * rows : (u + 1) * rows]
         d_centre[...] += total
-        d_neigh[...] += dot(oht[c], d_pre.astype(BF16))
-        return carry
-
-    lax.fori_loop(0, slots // CH, back, 0)
-
-    d_neigh_b = d_neigh[...].astype(BF16)
+        low = d_pre.astype(BF16)
+        first = low * left[here, :]
+        sides = jnp.concatenate([first, low - first], axis=1)
+        d_neigh[...] += dot(oht[c], sides)
+
+    for c in range(slots // CH):
+        back(c)
+
+    d_neigh_b = below(d_neigh[...]).astype(BF16)
     d_centre_b = d_centre[...].astype(BF16)
     moved = table[pl.ds(0, rows)]
     g_recv = inner(table[...], d_neigh_b)
@@ -445,6 +474,9 @@
         pltpu.SemaphoreType.REGULAR,
         pltpu.SemaphoreType.REGULAR,
         pltpu.SemaphoreType.REGULAR,
+        pltpu.VMEM((2 * width, 2 * width), BF16),
+        pltpu.VMEM((width, width), BF16),
+        pltpu.VMEM((edges, width), BF16),
         pltpu.VMEM((2, halo + 3 * migr, width), BF16),
         pltpu.VMEM((2, halo + 3 * migr, width), BF16),
         pltpu.VMEM((2, migr, width), BF16),
@@ -453,7 +485,7 @@
         pltpu.VMEM((2 * halo, width), BF16),
         pltpu.VMEM((slots, rows), jnp.int32),
         pltpu.VMEM((edges, table_rows), BF16),
-        pltpu.VMEM((slots // CH, table_rows, CH * rows), BF16),
+        pltpu.VMEM((slots // CH, table_rows // 2, CH * rows), BF16),
         pltpu.VMEM((edges, width), F32),
         pltpu.VMEM((table_rows, width), BF16),
         pltpu.VMEM((rows, width), F32),
@@ -463,7 +495,7 @@
         pltpu.VMEM((edges, width), F32),
         pltpu.VMEM((rows, width), F32),
         pltpu.VMEM((rows, width), F32),
-        pltpu.VMEM((table_rows, width), F32),
+        pltpu.VMEM((table_rows // 2, 2 * width), F32),
         pltpu.VMEM((width, width), F32),
     ]
     scratch += sum_scratch(plane, n_z, 3) + sum_scratch(plane, n_z, 3)

time: 47.2 us -> 44.8 us (0.949)
  Pallas kernels: 45 us -> 42.5 us
    pallas_call x1, Pallas kernels: 45 us -> 42.5 us  [shards(): pl.pallas_call(functools.partial(kernel, n_grp, n_y, n_z, (rows, slots, m...]
where the time goes in v5:
time: 44.8 us; the launch traced here: 44.6 us
  Pallas kernels  42.5 us (95%)
  local copies, waits for them, and re-layouts  1.41 us (3%)
  between operations  0.64 us (1%)
    pallas_call x1, Pallas kernels, shards(): pl.pallas_call(functools.partial(kernel, n_grp, n_y, n_z, (rows, slots, m...  42.5 us

profile of v5, /device:TPU:1, one launch (start us, length us, event | category | flops | bytes accessed | tf_op | source)
XLA Modules:
  0.0 44.6 jit_solution(5807733642247129603)
XLA Ops:
  0.6 42.5 %particle_step.1 = (bf16[2,256,128]{2,1,0:T(8,128)(2,1)S(1)}, f32[6,128,128]{2,1,0:T(8,128)S(1)}) custom-call(bf16[256,128]{1,0:T(8,128)(2,1)} %bitcast.8, s32[1,64]{1,0:T(1,128)} %refs_1_.1, s32[1,256]{1,0:T(1,128)} %refs_2_.1, s32[1,128]{1,0:T(1,128)} %refs_3_.1, s32[32,256]{1,0:T(8,128)} %bitcast.10, s32[32,256]{1,0:T(8,128)} %bitcast.11, ...), custom_call_target="tpu_custom_call" | custom-call | tf_op jit(solution)/shard_map/particle_step/pallas_call | solution.py:502
  43.2 0.7 %fusion = (bf16[1,256,128]{2,1,0:T(8,128)(2,1)}, bf16[1,256,128]{2,1,0:T(8,128)(2,1)}) fusion(bf16[2,256,128]{2,1,0:T(8,128)(2,1)S(1)} %get-tuple-element.5), kind=kLoop, calls=%fused_computation | loop fusion | bytes 262144 | tf_op jit(solution)/shard_map/slice | solution.py:516
  43.9 0.7 %copy.17 = f32[6,128,128]{2,1,0:T(8,128)} copy(f32[6,128,128]{2,1,0:T(8,128)S(1)} %get-tuple-element.14) | data formatting | bytes 786432

commit v6 on v5

--- a/solution.py
+++ b/solution.py
@@ -65,11 +65,11 @@
 
 
 class Sum:
-    def __init__(self, n_grp, n_y, n_z, mats, from_end, scratch):
+    def __init__(self, n_grp, n_y, n_z, mats, least, from_end, scratch):
         self.n_grp, self.n_y, self.n_z = n_grp, n_y, n_z
         self.mats = mats
         self.plane = n_grp * n_y
-        self.per, self.owners = shares(self.plane, mats)
+        self.per, self.owners = shares(self.plane, mats, least)
         self.offset = self.plane - self.owners if from_end else 0
         self.snd, self.rcv, self.part, self.zrcv, self.all, self.sems = scratch
         self.g = lax.axis_index("grp")
@@ -181,16 +181,16 @@
             out[first + m] = total / jnp.sqrt(square * (1.0 / (128 * 128)) + 1e-06)
 
 
-def shares(plane, mats):
+def shares(plane, mats, least):
     blocks = mats * 8
-    per = -(-blocks // plane)
+    per = max(-(-blocks // plane), least)
     while blocks % per:
         per += 1
     return per, blocks // per
 
 
-def sum_scratch(plane, n_z, mats):
-    per, owners = shares(plane, mats)
+def sum_scratch(plane, n_z, mats, least):
+    per, owners = shares(plane, mats, least)
     return [
         pltpu.VMEM((owners, per, 16, 128), BF16),
         pltpu.VMEM((plane, per, 16, 128), BF16),
@@ -201,6 +201,7 @@
     ]
 
 
+NO_EDGE = -1e30
 N_IN = 13
 CH = 16
 
@@ -329,7 +330,7 @@
         here = pl.ds(k * rows, rows)
         oh[here, :] = hot(index, (rows, table_rows), 1)
         index = jnp.broadcast_to(index, (rows, 128))
-        mask[here, :] = jnp.where(index < table_rows, 1.0, 0.0).astype(F32)
+        mask[here, :] = jnp.where(index < table_rows, 0.0, NO_EDGE).astype(F32)
         left[here, :] = jnp.where(index < middle, 1.0, 0.0).astype(BF16)
     for k in range(slots):
         index = row[k : k + 1, :]
@@ -364,10 +365,8 @@
         low = act.astype(BF16)
         hid[here, :] = low
         ds1[here, :] = slope
-        act, slope = silu_pair(below(dot(beside(low), w_pair[...])))
-        live = mask[here, :]
-        md[here, :] = live * slope
-        part = live * act
+        part, slope = silu_pair(below(dot(beside(low), w_pair[...])) + mask[here, :])
+        md[here, :] = slope
         total = part[0:rows]
         for u in range(1, CH):
             total = total + part[u * rows : (u + 1) * rows]
@@ -392,8 +391,8 @@
     g_agg = inner(agg_b, d_node_pre)
     if over_y:
         pl.semaphore_wait(y_sem, len(over_y))
-    early = Sum(n_grp, n_y, n_z, 3, False, reduce_scratch[:6])
-    late = Sum(n_grp, n_y, n_z, 3, True, reduce_scratch[6:])
+    early = Sum(n_grp, n_y, n_z, 3, 2, False, reduce_scratch[:6])
+    late = Sum(n_grp, n_y, n_z, 3, 1, True, reduce_scratch[6:])
     early.share([g_self, g_agg, g_out])
     d_local = cot[...].astype(F32) + by_transpose(d_node_pre, w_self[...])
 
@@ -498,7 +497,7 @@
         pltpu.VMEM((table_rows // 2, 2 * width), F32),
         pltpu.VMEM((width, width), F32),
     ]
-    scratch += sum_scratch(plane, n_z, 3) + sum_scratch(plane, n_z, 3)
+    scratch += sum_scratch(plane, n_z, 3, 2) + sum_scratch(plane, n_z, 3, 1)
     both, weight_steps = pl.pallas_call(
         functools.partial(kernel, n_grp, n_y, n_z, (rows, slots, migr, halo)),
         out_shape=(

time: 44.8 us -> 44.2 us (0.987)
  Pallas kernels: 42.5 us -> 41.9 us
    pallas_call x1, Pallas kernels: 42.5 us -> 41.9 us  [shards(): pl.pallas_call(functools.partial(kernel, n_grp, n_y, n_z, (rows, slots, m...]
where the time goes in v6:
time: 44.2 us; the launch traced here: 44 us
  Pallas kernels  41.9 us (95%)
  local copies, waits for them, and re-layouts  1.41 us (3%)
  between operations  0.64 us (1%)
    pallas_call x1, Pallas kernels, shards(): pl.pallas_call(functools.partial(kernel, n_grp, n_y, n_z, (rows, slots, m...  41.9 us

profile of v6, /device:TPU:1, one launch (start us, length us, event | category | flops | bytes accessed | tf_op | source)
XLA Modules:
  0.0 44.0 jit_solution(8856862783921882769)
XLA Ops:
  0.6 41.9 %particle_step.1 = (bf16[2,256,128]{2,1,0:T(8,128)(2,1)S(1)}, f32[6,128,128]{2,1,0:T(8,128)S(1)}) custom-call(bf16[256,128]{1,0:T(8,128)(2,1)} %bitcast.8, s32[1,64]{1,0:T(1,128)} %refs_1_.1, s32[1,256]{1,0:T(1,128)} %refs_2_.1, s32[1,128]{1,0:T(1,128)} %refs_3_.1, s32[32,256]{1,0:T(8,128)} %bitcast.10, s32[32,256]{1,0:T(8,128)} %bitcast.11, ...), custom_call_target="tpu_custom_call" | custom-call | tf_op jit(solution)/shard_map/particle_step/pallas_call | solution.py:501
  42.6 0.7 %fusion = (bf16[1,256,128]{2,1,0:T(8,128)(2,1)}, bf16[1,256,128]{2,1,0:T(8,128)(2,1)}) fusion(bf16[2,256,128]{2,1,0:T(8,128)(2,1)S(1)} %get-tuple-element.5), kind=kLoop, calls=%fused_computation | loop fusion | bytes 262144 | tf_op jit(solution)/shard_map/slice | solution.py:515
  43.2 0.7 %copy.17 = f32[6,128,128]{2,1,0:T(8,128)} copy(f32[6,128,128]{2,1,0:T(8,128)S(1)} %get-tuple-element.14) | data formatting | bytes 786432

commit v7 on v6

--- a/solution.py
+++ b/solution.py
@@ -203,7 +203,7 @@
 
 NO_EDGE = -1e30
 N_IN = 13
-CH = 16
+CH = 8
 
 
 def kernel(n_grp, n_y, n_z, dims, *refs):
@@ -222,6 +222,7 @@
         four_sem,
         w_pair,
         w_half,
+        table_t,
         left,
         snd,
         rcv,
@@ -243,8 +244,8 @@
         d_centre,
         d_neigh,
         g_msg,
-    ) = scratch[N_IN : N_IN + 28]
-    reduce_scratch = scratch[N_IN + 28 :]
+    ) = scratch[N_IN : N_IN + 29]
+    reduce_scratch = scratch[N_IN + 29 :]
     (nodes, leave, arrive, send, nbr, valid, w_send, w_recv, w_msg, w_self, w_agg, w_out, cot) = held
 
     g, slab = lax.axis_index("grp"), lax.axis_index("slab")
@@ -359,6 +360,8 @@
     span = CH * rows
 
     def front(c):
+        if c == 0:
+            table_t[...] = table[...].T
         here = pl.ds(c * span, span)
         pre = dot(oh[here, :], neigh[...]) + jnp.concatenate([centre[...]] * CH, axis=0)
         act, slope = silu_pair(pre)
@@ -387,7 +390,7 @@
     d_node_pre = (0.5 * d_hid * slope).astype(BF16)
     d_agg[...] = 0.5 * by_transpose(d_node_pre, w_agg[...])
     g_out = inner(node_hid, cot[...])
-    g_self = inner(moved, d_node_pre)
+    g_self = dot(table_t[:, 0:rows], d_node_pre)
     g_agg = inner(agg_b, d_node_pre)
     if over_y:
         pl.semaphore_wait(y_sem, len(over_y))
@@ -419,9 +422,8 @@
 
     d_neigh_b = below(d_neigh[...]).astype(BF16)
     d_centre_b = d_centre[...].astype(BF16)
-    moved = table[pl.ds(0, rows)]
-    g_recv = inner(table[...], d_neigh_b)
-    g_send = inner(moved, d_centre_b)
+    g_recv = dot(table_t[...], d_neigh_b)
+    g_send = dot(table_t[:, 0:rows], d_centre_b)
     late.share([g_send, g_recv, g_msg[...]])
     ret_snd[...] = by_transpose(d_neigh_b[rows:], w_recv[...]).astype(BF16)
     returning = [
@@ -475,6 +477,7 @@
         pltpu.SemaphoreType.REGULAR,
         pltpu.VMEM((2 * width, 2 * width), BF16),
         pltpu.VMEM((width, width), BF16),
+        pltpu.VMEM((width, table_rows), BF16),
         pltpu.VMEM((edges, width), BF16),
         pltpu.VMEM((2, halo + 3 * migr, width), BF16),
         pltpu.VMEM((2, halo + 3 * migr, width), BF16),

time: 44.2 us -> 43.8 us (level)
  no operation moved by 1% of the time
where the time goes in v7:
time: 43.8 us; the launch traced here: 43.6 us
  Pallas kernels  41.6 us (95%)
  local copies, waits for them, and re-layouts  1.41 us (3%)
  between operations  0.64 us (1%)
    pallas_call x1, Pallas kernels, shards(): pl.pallas_call(functools.partial(kernel, n_grp, n_y, n_z, (rows, slots, m...  41.6 us

profile of v7, /device:TPU:1, one launch (start us, length us, event | category | flops | bytes accessed | tf_op | source)
XLA Modules:
  0.0 43.6 jit_solution(17051037982746100863)
XLA Ops:
  0.6 41.6 %particle_step.1 = (bf16[2,256,128]{2,1,0:T(8,128)(2,1)S(1)}, f32[6,128,128]{2,1,0:T(8,128)S(1)}) custom-call(bf16[256,128]{1,0:T(8,128)(2,1)} %bitcast.8, s32[1,64]{1,0:T(1,128)} %refs_1_.1, s32[1,256]{1,0:T(1,128)} %refs_2_.1, s32[1,128]{1,0:T(1,128)} %refs_3_.1, s32[32,256]{1,0:T(8,128)} %bitcast.10, s32[32,256]{1,0:T(8,128)} %bitcast.11, ...), custom_call_target="tpu_custom_call" | custom-call | tf_op jit(solution)/shard_map/particle_step/pallas_call | solution.py:504
  42.2 0.7 %fusion = (bf16[1,256,128]{2,1,0:T(8,128)(2,1)}, bf16[1,256,128]{2,1,0:T(8,128)(2,1)}) fusion(bf16[2,256,128]{2,1,0:T(8,128)(2,1)S(1)} %get-tuple-element.5), kind=kLoop, calls=%fused_computation | loop fusion | bytes 262144 | tf_op jit(solution)/shard_map/slice | solution.py:518
  42.9 0.7 %copy.17 = f32[6,128,128]{2,1,0:T(8,128)} copy(f32[6,128,128]{2,1,0:T(8,128)S(1)} %get-tuple-element.14) | data formatting | bytes 786432
